TPU v7x, 256 devices: a whole 4x4x8 slice. The times are simulated.
256 devices in a mesh: gz: 4 (over y), row: 8 (over x, core), col: 8 (over z).
Axes of the slice: x: 4, y: 4, z: 8, core: 2. Of those that a mesh axis runs over, the one named last changes fastest.
Arguments:
- front_in: bfloat16 [4, 16384, 8192], P('gz', 'row', 'col'), may hold values from -6 to 6
- pattern: int32 [4, 64, 32], P('gz', 'row', 'col'), may hold values 0 or 1
- lower_inv: float32 [4, 2, 256, 256], P('gz'), as said below
- upper_inv: float32 [4, 2, 256, 256], P('gz'), as said below
- targets: int32 [4, 16384], P('gz', 'row'), may hold values from 0 to 65535, as said below
Outputs:
- lower_fac: bfloat16 [4, 16384, 512], P('gz', 'row')
- upper_fac: bfloat16 [4, 512, 8192], P('gz', None, 'col')
- ancestor: float32 [65536, 8192], P(('gz', 'row'), 'col')
Inputs may be any that keep to these rules, and one draw needn't show every extreme that they name: Within one group the targets of rows 512 and beyond are distinct. Take the ancestor rows in shards of 2048 rows, shard p holding rows p * 8 * 256 onward: among the 2048 rows of a group that one index of row holds, at most 96 have targets in one shard, and exactly 96 in half of the shards. lower_inv[g, k] is lower triangular with a positive diagonal. upper_inv[g, k] is upper triangular with a positive diagonal.
All inputs are finite; a program needn't handle non-finite values. No bound on the sum of `pattern` on one device may be relied on, other than what follows from the above.
Results may differ from a plain program's by a relative error of at most 0.0032.
Values may be sent and summed in bfloat16 or wider, within the bound.
No kernel may reach another device: no remote copies, remote signals or barrier semaphores. Data moves between devices by JAX's collectives and lax.ppermute only.
A program may use at most 128 MiB of HBM per device.

v0:
```python
import jax
import jax.numpy as jnp
from jax import lax
from jax.sharding import PartitionSpec as P


def from_root(block, axis, owner):
    block = jnp.where(lax.axis_index(axis) == owner, block, jnp.zeros_like(block))
    return lax.psum(block, axis)


def expand(matrix, pattern_f, block_size):
    rows_n, cols_n = matrix.shape
    shaped = matrix.reshape(rows_n // block_size, block_size, cols_n // block_size, block_size)
    return (shaped * pattern_f[:, None, :, None]).reshape(rows_n, cols_n)


def local(front_in, pattern, lower_inv, upper_inv, targets):
    highest = lax.Precision.HIGHEST
    block_size = lower_inv.shape[-1]
    rows_local = front_in.shape[1]
    col_width = front_in.shape[2]
    row_count = rows_local // block_size
    col_count = col_width // block_size
    pattern_f = pattern[0].astype(jnp.float32)
    row_block = lax.axis_index("row") * row_count + jnp.arange(rows_local) // block_size
    col_block = lax.axis_index("col") * col_count + jnp.arange(col_width) // block_size
    matrix = expand(front_in[0].astype(jnp.float32), pattern_f, block_size)

    def panels(current, step_level):
        lower_panel = jnp.dot(
            current[:, step_level * block_size : (step_level + 1) * block_size],
            upper_inv[0, step_level],
            precision=highest,
            preferred_element_type=jnp.float32,
        )
        lower_panel = jnp.where(
            (row_block > step_level)[:, None], lower_panel, jnp.float32(0.0)
        ).astype(jnp.bfloat16)
        upper_panel = jnp.dot(
            lower_inv[0, step_level],
            current[step_level * block_size : (step_level + 1) * block_size, :],
            precision=highest,
            preferred_element_type=jnp.float32,
        )
        upper_panel = jnp.where(
            (col_block > step_level)[None, :], upper_panel, jnp.float32(0.0)
        ).astype(jnp.bfloat16)
        lower_b = from_root(lower_panel, "col", 0)
        upper_b = from_root(upper_panel, "row", 0)
        return (lower_b, upper_b)

    def update(current, lower_b, upper_b):
        product = jnp.dot(lower_b, upper_b, preferred_element_type=jnp.float32)
        return current - expand(product, pattern_f, block_size)

    lower_zero, upper_zero = panels(matrix, 0)
    matrix = update(matrix, lower_zero, upper_zero)
    lower_one, upper_one = panels(matrix, 1)
    matrix = update(matrix, lower_one, upper_one)
    lower_fac = jnp.concatenate([lower_zero, lower_one], axis=1)[None]
    upper_fac = jnp.concatenate([upper_zero, upper_one], axis=0)[None]
    keep_mask = (row_block >= 2)[:, None] & (col_block >= 2)[None, :]
    contribution = jnp.where(keep_mask, matrix, jnp.float32(0.0)).astype(jnp.bfloat16)
    group_count = lax.axis_size("gz")
    grid_rows = lax.axis_size("row")
    peer_count = group_count * grid_rows
    capacity = 3 * rows_local // (2 * peer_count)
    target_rows = targets[0]
    peer_id = target_rows // rows_local
    local_row = target_rows % rows_local
    valid_rows = row_block >= 2
    one_hot = ((peer_id[:, None] == jnp.arange(peer_count)[None, :]) & valid_rows[:, None]).astype(
        jnp.int32
    )
    running = jnp.cumsum(one_hot, axis=0) - 1
    slot_rank = jnp.sum(one_hot * running, axis=1)
    slot_dest = jnp.where(valid_rows, peer_id * capacity + slot_rank, peer_count * capacity)
    send_rows = (
        jnp.zeros((peer_count * capacity, col_width), jnp.bfloat16)
        .at[slot_dest]
        .set(contribution, mode="drop")
    )
    send_index = (
        jnp.full((peer_count * capacity,), rows_local, jnp.int32)
        .at[slot_dest]
        .set(local_row, mode="drop")
    )
    got_rows, got_index = (
        lax.all_to_all(
            send_rows.reshape(peer_count, capacity, col_width),
            ("gz", "row"),
            split_axis=0,
            concat_axis=0,
            tiled=True,
        ),
        lax.all_to_all(
            send_index.reshape(peer_count, capacity),
            ("gz", "row"),
            split_axis=0,
            concat_axis=0,
            tiled=True,
        ),
    )
    ancestor = (
        jnp.zeros((rows_local, col_width), jnp.float32)
        .at[got_index.reshape(-1)]
        .add(got_rows.reshape(-1, col_width).astype(jnp.float32), mode="drop")
    )
    return (lower_fac, upper_fac, ancestor)


def solution(mesh):
    return jax.shard_map(
        local,
        mesh=mesh,
        in_specs=(
            P("gz", "row", "col"),
            P("gz", "row", "col"),
            P("gz", None, None, None),
            P("gz", None, None, None),
            P("gz", "row"),
        ),
        out_specs=(P("gz", "row", None), P("gz", None, "col"), P(("gz", "row"), "col")),
        check_vma=False,
    )
```

profile of v0, /device:TPU:96, one launch (start us, length us, event | category | flops | bytes accessed | tf_op | source)
XLA Modules:
  0.0 467.4 jit_solution(3997023929928631108)
XLA Ops:
  7.2 0.0 all-reduce.7.cloned.1.call-start
  7.2 0.7 convert_bitcast_fusion
  7.9 0.1 copy.10
  8.0 0.0 copy-start.6
  8.0 8.9 %reshape.274 = f32[8,256,4,256]{3,2,1,0:T(4,128)} reshape(bf16[1,2048,1024]{2,1,0:T(8,128)(2,1)} %param.5) | data formatting | bytes 12582912 | tf_op jit(solution)/shard_map/convert_element_type | solution.py:28
  16.9 1.5 slice_multiply_fusion
  18.3 0.2 copy.16
  18.5 0.0 copy-done.6
  18.6 2.6 fusion.16
  21.2 0.0 all-reduce.7.cloned.1.call-update
  21.2 0.0 all-reduce.5.cloned.1.call-start
  21.3 4.5 mul.50
  25.8 0.0 copy-start.2
  25.8 5.6 %copy.15 = f32[256,8,4,256]{3,1,2,0:T(8,128)S(1)} copy(f32[256,8,4,256]{3,2,1,0:T(4,128)} %bitcast.74) | data formatting | bytes 16777216
  31.5 0.0 copy-start
  31.5 0.0 copy-done.2
  31.5 0.0 copy-start.5
  31.5 0.0 copy-start.7
  31.5 5.1 %bitcast_multiply_fusion = f32[2048,1024]{1,0:T(8,128)} fusion(f32[2048,1024]{1,0:T(8,128)S(1)} %bitcast.71, bf16[1,2048,1024]{2,1,0:T(8,128)(2,1)S(1)} %copy-done.2), kind=kLoop, calls=%fused_computation.5 | loop fusion | flops 4194304 | bytes 20971520 | tf_op jit(solution)/shard_map/mul | solution.py:15
  36.6 0.8 copy-done
  37.4 0.0 copy-done.5
  37.4 4.4 fusion.8
  41.8 0.0 all-reduce.5.cloned.1.call-update
  41.8 0.2 all-reduce.11.cloned.1.call-start
  42.1 0.0 copy-done.7
  42.2 46.8 %all-reduce.7.cloned.1.call-done = bf16[256,1024]{0,1:T(8,128)(2,1)} async-done(((bf16[256,1024]{0,1:T(8,128)(2,1)}), bf16[256,1024]{0,1:T(8,128)(2,1)}) %all-reduce.7.cloned.1.call-update) | async-done | bytes 524304 | tf_op jit(solution)/shard_map/psum | solution.py:9
  89.0 77.3 %all-reduce.5.cloned.1.call-done = bf16[2048,256]{1,0:T(8,128)(2,1)} async-done(((bf16[2048,256]{1,0:T(8,128)(2,1)}), bf16[2048,256]{1,0:T(8,128)(2,1)}) %all-reduce.5.cloned.1.call-update) | async-done | bytes 1048592 | tf_op jit(solution)/shard_map/psum | solution.py:9
  166.3 6.4 %multiply_subtract_fusion = f32[2048,1024]{1,0:T(8,128)S(1)} fusion(f32[2048,1024]{1,0:T(8,128)} %bitcast.72, bf16[2048,256]{1,0:T(8,128)(2,1)} %all-reduce.5.cloned.1.call-done, bf16[256,1024]{0,1:T(8,128)(2,1)} %all-reduce.7.cloned.1.call-done, bf16[1,2048,1024]{2,1,0:T(8,128)(2,1)} %param.5), kind=kOutput, calls=%fused_computation.7 | convolution fusion | flops 1082130432 | bytes 22544384 | tf_op jit(solution)/shard_map/dot_general | solution.py:54
  172.7 0.0 copy-start.1
  172.7 3.2 copy-done.1
  175.9 2.7 fusion.14
  178.6 0.0 all-reduce.11.cloned.1.call-update
  178.6 0.0 all-reduce.9.cloned.1.call-start
  178.7 4.4 fusion.7
  183.1 0.0 all-reduce.9.cloned.1.call-update
  183.1 9.1 %reduce-window.6 = s32[32,16,128]{2,1,0:T(8,128)S(1)} reduce-window(s32[32,16,128]{2,1,0:T(8,128)S(1)} %fusion.30, s32[]{:T(128)} %constant.88.clone.1), window={size=1x1x128 pad=0_0x0_0x127_0}, to_apply=%region_4.5 | reduce-window | flops 8323072 | bytes 524292 | tf_op jit(solution)/shard_map/reduce-window
  192.2 0.1 slice.49
  192.3 0.2 copy.14
  192.6 0.2 reduce-window.9
  192.8 0.1 add_add_fusion
  192.9 0.1 fusion.19
  193.0 0.1 compare_select_fusion.1
  193.1 8.1 %scatter_custom_fusion = s32[3072]{0:T(1024)S(1)} fusion(s32[2048]{0:T(1024)S(1)} %bitcast.85, s32[2048]{0:T(1024)S(1)} %get-tuple-element.9, s32[]{:T(128)} %constant.97.clone.1), kind=kCustom, calls=%fused_computation.96 | custom fusion | bytes 12292 | tf_op jit(solution)/shard_map/scatter | solution.py:87
  201.2 0.7 all_to_all.9
  201.9 7.3 %all-to-all-start = ((s32[32,1,96]{2,1,0:T(1,128)}), s32[32,1,96]{2,1,0:T(1,128)S(1)}, u32[]{:S(2)}, u32[]{:S(2)}) async-start(s32[32,1,96]{2,1,0:T(1,128)} %all_to_all.9), calls=%async_computation | async-start | bytes 32768 | tf_op jit(solution)/shard_map/all_to_all | solution.py:97
  209.2 34.8 %all-reduce.11.cloned.1.call-done = bf16[256,1024]{0,1:T(8,128)(2,1)} async-done(((bf16[256,1024]{0,1:T(8,128)(2,1)}), bf16[256,1024]{0,1:T(8,128)(2,1)}) %all-reduce.11.cloned.1.call-update) | async-done | bytes 524304 | tf_op jit(solution)/shard_map/psum | solution.py:9
  244.0 77.0 %all-reduce.9.cloned.1.call-done = bf16[2048,256]{1,0:T(8,128)(2,1)} async-done(((bf16[2048,256]{1,0:T(8,128)(2,1)}), bf16[2048,256]{1,0:T(8,128)(2,1)}) %all-reduce.9.cloned.1.call-update) | async-done | bytes 1048592 | tf_op jit(solution)/shard_map/psum | solution.py:9
  321.0 10.0 %select_convert_fusion = bf16[2048,1024]{1,0:T(8,128)(2,1)} fusion(f32[2048,1024]{1,0:T(8,128)} %copy-done.1, f32[2048,1024]{1,0:T(8,128)} %bitcast.73, bf16[2048,256]{1,0:T(8,128)(2,1)} %all-reduce.9.cloned.1.call-done, bf16[256,1024]{0,1:T(8,128)(2,1)} %all-reduce.11.cloned.1.call-done, pred[1024]{0:T(1024)(128)(4,1)S(1)} %fusion.51, ...), kind=kOutput, calls=%fused_computation.6 | convolution fusion | flops 1084227584 | bytes 22547456 | tf_op jit(solution)/shard_map/dot_general | solution.py:54
  331.0 14.3 %scatter_custom_fusion.1 = bf16[3072,1024]{1,0:T(8,128)(2,1)} fusion(s32[2048]{0:T(1024)S(1)} %bitcast.86, bf16[2048,1024]{1,0:T(8,128)(2,1)} %select_convert_fusion, bf16[]{:T(256)} %constant.95.clone.1), kind=kCustom, calls=%fused_computation.9 | custom fusion | bytes 6291968 | tf_op jit(solution)/shard_map/scatter | solution.py:82
  345.3 0.0 all-to-all-done
  345.3 0.0 copy-start.3
  345.3 0.0 copy-start.4
  345.3 7.6 %all-to-all-start.1 = ((bf16[32,96,1024]{2,1,0:T(8,128)(2,1)}), bf16[32,96,1024]{2,1,0:T(8,128)(2,1)}, u32[]{:S(2)}, u32[]{:S(2)}) async-start(bf16[32,96,1024]{2,1,0:T(8,128)(2,1)} %bitcast.75), calls=%async_computation.1 | async-start | bytes 12582912 | tf_op jit(solution)/shard_map/all_to_all | solution.py:90
  352.9 0.5 broadcast.462
  353.4 0.7 reduce.3
  354.1 0.1 reshape.271
  354.2 1.3 maximum_bitcast_fusion.1
  355.5 1.3 copy.13
  356.8 0.0 copy-done.3
  356.8 0.0 copy-done.4
  356.8 1.5 maximum_bitcast_fusion
  358.3 72.2 %all-to-all-done.1 = bf16[32,96,1024]{2,1,0:T(8,128)(2,1)} async-done(((bf16[32,96,1024]{2,1,0:T(8,128)(2,1)}), bf16[32,96,1024]{2,1,0:T(8,128)(2,1)}, u32[]{:S(2)}, u32[]{:S(2)}) %all-to-all-start.1) | async-done | bytes 6291488 | tf_op jit(solution)/shard_map/all_to_all | solution.py:90
  430.5 30.4 %scatter_custom_fusion.2 = f32[2048,1024]{1,0:T(8,128)} fusion(s32[3072]{0:T(1024)S(1)} %bitcast.84, bf16[3072,1024]{1,0:T(8,128)(2,1)} %bitcast.21, f32[]{:T(128)} %constant.94.clone.1), kind=kCustom, calls=%fused_computation.3 | custom fusion | flops 6291456 | bytes 14680068 | tf_op jit(solution)/shard_map/scatter-add | solution.py:108
  (12 shorter events, 0.1 us)
Async XLA Ops:
  7.2 81.8 %all-reduce.7.cloned.1.call-start = ((), (), s32[]{:S(2)}) async-start(), calls=%async_computation.3 | async-start | bytes 1048576 | tf_op jit(solution)/shard_map/psum | solution.py:9
  8.0 10.6 %copy-start.6 = (f32[1,2,256,256]{3,2,1,0:T(8,128)S(1)}, f32[1,2,256,256]{3,2,1,0:T(8,128)}, u32[]{:S(2)}) copy-start(f32[1,2,256,256]{3,2,1,0:T(8,128)} %param.7) | copy-start | bytes 1572868
  21.2 145.0 %all-reduce.5.cloned.1.call-start = ((), (), s32[]{:S(2)}) async-start(), calls=%async_computation.2 | async-start | bytes 2097152 | tf_op jit(solution)/shard_map/psum | solution.py:9
  25.8 5.7 %copy-start.2 = (bf16[1,2048,1024]{2,1,0:T(8,128)(2,1)S(1)}, bf16[1,2048,1024]{2,1,0:T(8,128)(2,1)}, u32[]{:S(2)}) copy-start(bf16[1,2048,1024]{2,1,0:T(8,128)(2,1)} %param.5) | copy-start | bytes 12582916
  31.5 5.9 %copy-start = (f32[256,8,4,256]{3,1,2,0:T(8,128)}, f32[256,8,4,256]{3,1,2,0:T(8,128)S(1)}, u32[]{:S(2)}) copy-start(f32[256,8,4,256]{3,1,2,0:T(8,128)S(1)} %copy.15) | copy-start | bytes 25165828
  31.5 5.9 %copy-start.5 = (f32[1,2,256,256]{3,2,1,0:T(8,128)S(1)}, f32[1,2,256,256]{3,2,1,0:T(8,128)}, u32[]{:S(2)}) copy-start(f32[1,2,256,256]{3,2,1,0:T(8,128)} %param.8) | copy-start | bytes 1572868
  31.5 10.6 %copy-start.7 = (s32[1,2048]{1,0:T(1,128)S(1)}, s32[1,2048]{1,0:T(1,128)}, u32[]{:S(2)}) copy-start(s32[1,2048]{1,0:T(1,128)} %param.9) | copy-start | bytes 24580
  41.8 202.2 %all-reduce.11.cloned.1.call-start = ((), (), s32[]{:S(2)}) async-start(), calls=%async_computation.5 | async-start | bytes 1048576 | tf_op jit(solution)/shard_map/psum | solution.py:9
  172.7 3.2 copy-start.1
  178.6 142.4 %all-reduce.9.cloned.1.call-start = ((), (), s32[]{:S(2)}) async-start(), calls=%async_computation.4 | async-start | bytes 2097152 | tf_op jit(solution)/shard_map/psum | solution.py:9
  201.9 143.4 %all-to-all-start = ((s32[32,1,96]{2,1,0:T(1,128)}), s32[32,1,96]{2,1,0:T(1,128)S(1)}, u32[]{:S(2)}, u32[]{:S(2)}) async-start(s32[32,1,96]{2,1,0:T(1,128)} %all_to_all.9), calls=%async_computation | async-start | bytes 32768 | tf_op jit(solution)/shard_map/all_to_all | solution.py:97
  345.3 11.5 %copy-start.3 = (bf16[2048,256]{1,0:T(8,128)(2,1)S(1)}, bf16[2048,256]{1,0:T(8,128)(2,1)}, u32[]{:S(2)}) copy-start(bf16[2048,256]{1,0:T(8,128)(2,1)} %all-reduce.5.cloned.1.call-done) | copy-start | bytes 3145732
  345.3 11.5 %copy-start.4 = (bf16[2048,256]{1,0:T(8,128)(2,1)S(1)}, bf16[2048,256]{1,0:T(8,128)(2,1)}, u32[]{:S(2)}) copy-start(bf16[2048,256]{1,0:T(8,128)(2,1)} %all-reduce.9.cloned.1.call-done) | copy-start | bytes 3145732
  345.3 85.2 %all-to-all-start.1 = ((bf16[32,96,1024]{2,1,0:T(8,128)(2,1)}), bf16[32,96,1024]{2,1,0:T(8,128)(2,1)}, u32[]{:S(2)}, u32[]{:S(2)}) async-start(bf16[32,96,1024]{2,1,0:T(8,128)(2,1)} %bitcast.75), calls=%async_computation.1 | async-start | bytes 12582912 | tf_op jit(solution)/shard_map/all_to_all | solution.py:90
Sparse Core Ops, SparseCore 0:
  21.3 67.5 all-reduce.6
  92.0 74.2 all-reduce.4
  178.8 65.2 all-reduce.10
  246.8 74.1 all-reduce.8
where the time goes:
time: 469 us; the launch traced here: 467 us
  waiting for transfers between devices  308 us (66%)
  other arithmetic  50.7 us (11%)
  local copies, waits for them, and re-layouts  48.7 us (10%)
  matrix products  30.5 us (7%)
  starting transfers between devices  15.3 us (3%)
  between operations  14 us (3%)
    psum x4, waiting for transfers between devices, from_root(): return lax.psum(block, axis)  236 us
    all_to_all x1, waiting for transfers between devices, local(): lax.all_to_all(send_rows.reshape(peer_count, capacity, col_width), ('gz',...  72.2 us
    scatter-add x1, other arithmetic, local(): ancestor = jnp.zeros((rows_local, col_width), jnp.float32).at[got_index.r...  30.4 us
    dot_general x2, matrix products, update(): product = jnp.dot(lower_b, upper_b, preferred_element_type=jnp.float32)  16.4 us
    scatter x1, local copies, waits for them, and re-layouts, local(): send_rows = jnp.zeros((peer_count * capacity, col_width), jnp.bfloat16).a...  14.3 us
    unnamed x19, local copies, waits for them, and re-layouts  11.2 us
  transfers between devices with their start and end apart: 6, of which 5 were waited for; matrix products, arithmetic and copies ran while one was open for 15% of the time, Pallas kernels for 0%

commit v1 on v0

v1 whole, which is shorter than its diff:
```python
import jax
import jax.numpy as jnp
from jax import lax
from jax.experimental import pallas as pl
from jax.experimental.pallas import tpu as pltpu
from jax.sharding import PartitionSpec as P

BF = jnp.bfloat16
F32 = jnp.float32
B = 256
CAP = 96
VMEM_LIMIT = 48 * 2**20


def params():
    return pltpu.CompilerParams(vmem_limit_bytes=VMEM_LIMIT)


def mm(a, b):
    return jnp.dot(a, b, preferred_element_type=F32)


def split(a):
    hi = a.astype(BF)
    return hi, (a - hi.astype(F32)).astype(BF)


def dot_split(a, b):
    ah, al = split(a)
    bh, bl = split(b)
    return mm(ah, bh) + (mm(ah, bl) + mm(al, bh))


def panels_zero_kernel(pos_ref, pat_ref, cols_ref, rows_ref, li_ref, ui_ref, l_ref, u_ref):
    n_row, n_col = l_ref.shape[0] // B, u_ref.shape[1] // B
    row0, col0 = pos_ref[0] * n_row, pos_ref[1] * n_col
    uh, ul = split(ui_ref[0, 0])
    lh, ll = split(li_ref[0, 0])
    for i in range(n_row):
        keep = jnp.where(row0 + i > 0, pat_ref[i, 0], 0).astype(F32)
        block = cols_ref[0, i * B : (i + 1) * B, 0:B]
        l_ref[i * B : (i + 1) * B, :] = ((mm(block, uh) + mm(block, ul)) * keep).astype(BF)
    for j in range(n_col):
        keep = jnp.where(col0 + j > 0, pat_ref[0, j], 0).astype(F32)
        block = rows_ref[0, 0:B, j * B : (j + 1) * B]
        u_ref[:, j * B : (j + 1) * B] = ((mm(lh, block) + mm(ll, block)) * keep).astype(BF)


def panels_one_kernel(
    pos_ref, pat_ref, cols_ref, rows_ref, li_ref, ui_ref, l0_ref, u0_ref, uc_ref, lc_ref, l_ref, u_ref
):
    n_row, n_col = l_ref.shape[0] // B, u_ref.shape[1] // B
    row0, col0 = pos_ref[0] * n_row, pos_ref[1] * n_col
    ui, li = ui_ref[0, 1], li_ref[0, 1]
    for i in range(n_row):
        keep = jnp.where(row0 + i > 1, pat_ref[i, 1], 0).astype(F32)
        rows = slice(i * B, (i + 1) * B)
        block = cols_ref[0, rows, B : 2 * B].astype(F32) - mm(l0_ref[rows, :], uc_ref[...])
        l_ref[rows, :] = (dot_split(block, ui) * keep).astype(BF)
    for j in range(n_col):
        keep = jnp.where(col0 + j > 1, pat_ref[1, j], 0).astype(F32)
        cols = slice(j * B, (j + 1) * B)
        block = rows_ref[0, B : 2 * B, cols].astype(F32) - mm(lc_ref[...], u0_ref[:, cols])
        u_ref[:, cols] = (dot_split(li, block) * keep).astype(BF)


def slots_kernel(pos_ref, targets_ref, slot_ref, value_ref):
    rows = targets_ref.shape[1]
    peers = 32
    target = targets_ref[...]
    peer = target // rows
    local = target - peer * rows
    row_id = pos_ref[0] * rows + lax.broadcasted_iota(jnp.int32, (1, rows), 1)
    valid = row_id >= 2 * B
    ids = lax.broadcasted_iota(jnp.int32, (peers, rows), 0)
    hot = jnp.where((ids == peer) & valid, 1.0, 0.0)
    before = jnp.where(
        lax.broadcasted_iota(jnp.int32, (B, B), 0) < lax.broadcasted_iota(jnp.int32, (B, B), 1), 1.0, 0.0
    ).astype(BF)
    seen = jnp.zeros((peers, 1), F32)
    for i in range(rows // B):
        part = hot[:, i * B : (i + 1) * B]
        rank = mm(part.astype(BF), before) + seen
        seen = seen + jnp.sum(part, axis=1, keepdims=True)
        place = rank + (CAP * ids[:, i * B : (i + 1) * B]).astype(F32)
        slot = jnp.sum(part * place, axis=0, keepdims=True).astype(jnp.int32)
        ok = valid[:, i * B : (i + 1) * B]
        slot_ref[:, i * B : (i + 1) * B] = jnp.where(ok, slot, -1)
    high = local // 64
    which = lax.broadcasted_iota(jnp.int32, (16, rows), 0)
    value = jnp.where(which == 0, high, jnp.where(which == 1, local - high * 64, jnp.where(which == 2, 1, 0)))
    value_ref[...] = value.astype(F32).astype(BF)


def one_hot(first, count, slot):
    ids = first + lax.broadcasted_iota(jnp.int32, (count, slot.shape[1]), 0)
    return jnp.where(ids == slot, 1.0, 0.0).astype(BF)


def pack_kernel(slot_ref, value_ref, front_ref, pat_ref, rows_ref, keep_ref, index_ref):
    count = rows_ref.shape[0]
    hot = one_hot(pl.program_id(0) * count, count, slot_ref[...])
    keep = mm(hot, pat_ref[...])
    keep_ref[...] = keep.astype(BF)
    for j in range(rows_ref.shape[1] // B):
        cols = slice(j * B, (j + 1) * B)
        rows_ref[:, cols] = (mm(hot, front_ref[0, :, cols]) * keep[:, j : j + 1]).astype(BF)
    info = lax.dot_general(value_ref[...], hot, (((1,), (1,)), ((), ())), preferred_element_type=F32)
    index = info[0:1] * 64.0 + info[1:2] + (1.0 - info[2:3]) * 4096.0
    index_ref[...] = jnp.broadcast_to(index, (8, count)).astype(jnp.int32)


def update_kernel(slot_ref, lower_ref, u0_ref, u1_ref, rows_ref, keep_ref, out_ref):
    count = rows_ref.shape[0]
    hot = one_hot(pl.program_id(0) * count, count, slot_ref[...])
    low = mm(hot, lower_ref[...]).astype(BF)
    for j in range(rows_ref.shape[1] // B):
        cols = slice(j * B, (j + 1) * B)
        product = mm(low[:, 0:B], u0_ref[:, cols]) + mm(low[:, B : 2 * B], u1_ref[:, cols])
        keep = keep_ref[:, j : j + 1].astype(F32)
        out_ref[:, cols] = (rows_ref[:, cols].astype(F32) - product * keep).astype(BF)


def add_kernel(index_ref, got_ref, out_ref):
    hot = one_hot(pl.program_id(0) * out_ref.shape[0], out_ref.shape[0], index_ref[...])
    out_ref[...] = mm(hot, got_ref[...])


def whole(shape):
    return pl.BlockSpec(shape, lambda *_: (0,) * len(shape))


SMEM = pl.BlockSpec(memory_space=pltpu.SMEM)
TREE = (((0, 4),), ((0, 2), (4, 6)), ((0, 1), (2, 3), (4, 5), (6, 7)))


def tree(block, axis):
    block = jnp.where(lax.axis_index(axis) == 0, block, jnp.zeros_like(block))
    for pairs in TREE:
        block = block + lax.ppermute(block, axis, pairs)
    return block


def spread(lower, axis):
    n = lax.axis_size(axis)
    rows = lower.shape[0] // n
    piece = jnp.where(lax.axis_index(axis) == 0, lower[:rows], jnp.zeros_like(lower[:rows]))
    for c in range(1, n):
        piece = piece + lax.ppermute(lower[c * rows : (c + 1) * rows], axis, [(0, c)])
    return lax.all_gather(piece, axis, axis=0, tiled=True)


def local(front_in, pattern, lower_inv, upper_inv, targets):
    rows, width = front_in.shape[1:]
    n_col = width // B
    peers = lax.axis_size("gz") * lax.axis_size("row")
    slots = peers * CAP
    pos = jnp.stack([lax.axis_index("row"), lax.axis_index("col")]).astype(jnp.int32)
    pat = pattern[0]
    part = slots // 4

    cols_spec = pl.BlockSpec((1, rows, 2 * B), lambda *_: (0, 0, 0))
    rows_spec = pl.BlockSpec((1, 2 * B, width), lambda *_: (0, 0, 0))
    inv_spec = whole((1, 2, B, B))
    shapes = (jax.ShapeDtypeStruct((rows, B), BF), jax.ShapeDtypeStruct((B, width), BF))
    l0, u0 = pl.pallas_call(
        panels_zero_kernel,
        grid=(1,),
        in_specs=[SMEM, SMEM, cols_spec, rows_spec, inv_spec, inv_spec],
        out_specs=[whole((rows, B)), whole((B, width))],
        out_shape=shapes,
        compiler_params=params(),
        name="panels_zero",
    )(pos, pat, front_in, front_in, lower_inv, upper_inv)
    upper_corner = tree(u0[:, B : 2 * B], "row")
    lower_corner = tree(l0[B : 2 * B], "col")
    l1, u1 = pl.pallas_call(
        panels_one_kernel,
        grid=(1,),
        in_specs=[SMEM, SMEM, cols_spec, rows_spec, inv_spec, inv_spec]
        + [whole((rows, B)), whole((B, width)), whole((B, B)), whole((B, B))],
        out_specs=[whole((rows, B)), whole((B, width))],
        out_shape=shapes,
        compiler_params=params(),
        name="panels_one",
    )(pos, pat, front_in, front_in, lower_inv, upper_inv, l0, u0, upper_corner, lower_corner)

    slot, value = pl.pallas_call(
        slots_kernel,
        in_specs=[SMEM, pl.BlockSpec(memory_space=pltpu.VMEM)],
        out_shape=(jax.ShapeDtypeStruct((1, rows), jnp.int32), jax.ShapeDtypeStruct((16, rows), BF)),
        name="slots",
    )(pos, targets)
    keep_col = (pos[1] * n_col + jnp.arange(n_col)) >= 2
    keep_pat = jnp.where(keep_col[None, :], pat, 0).astype(BF)
    pat_rows = jnp.pad(jnp.repeat(keep_pat, B, axis=0), ((0, 0), (0, 128 - n_col)))
    packed, keep, index = pl.pallas_call(
        pack_kernel,
        grid=(4,),
        in_specs=[whole((1, rows)), whole((16, rows)), whole((1, rows, width)), whole((rows, 128))],
        out_specs=[
            pl.BlockSpec((part, width), lambda i: (i, 0)),
            pl.BlockSpec((part, 128), lambda i: (i, 0)),
            pl.BlockSpec((8, part), lambda i: (0, i)),
        ],
        out_shape=(
            jax.ShapeDtypeStruct((slots, width), BF),
            jax.ShapeDtypeStruct((slots, 128), BF),
            jax.ShapeDtypeStruct((8, slots), jnp.int32),
        ),
        compiler_params=params(),
        name="pack",
    )(slot, value, front_in, pat_rows)
    got_index = lax.all_to_all(
        index[0].reshape(peers, CAP), ("gz", "row"), split_axis=0, concat_axis=0, tiled=True
    ).reshape(1, slots)

    upper_zero = tree(u0, "row")
    upper_one = tree(u1, "row")
    lower = spread(jnp.concatenate([l0, l1], axis=1), "col")

    send = pl.pallas_call(
        update_kernel,
        grid=(4,),
        in_specs=[
            whole((1, rows)),
            whole((rows, 2 * B)),
            whole((B, width)),
            whole((B, width)),
            pl.BlockSpec((part, width), lambda i: (i, 0)),
            pl.BlockSpec((part, 128), lambda i: (i, 0)),
        ],
        out_specs=pl.BlockSpec((part, width), lambda i: (i, 0)),
        out_shape=jax.ShapeDtypeStruct((slots, width), BF),
        compiler_params=params(),
        name="update",
    )(slot, lower, upper_zero, upper_one, packed, keep)
    got = lax.all_to_all(
        send.reshape(peers, CAP, width), ("gz", "row"), split_axis=0, concat_axis=0, tiled=True
    ).reshape(slots, width)
    ancestor = pl.pallas_call(
        add_kernel,
        grid=(8,),
        in_specs=[whole((1, slots)), whole((slots, width))],
        out_specs=pl.BlockSpec((rows // 8, width), lambda i: (i, 0)),
        out_shape=jax.ShapeDtypeStruct((rows, width), F32),
        compiler_params=params(),
        name="add",
    )(got_index, got)
    upper = jnp.concatenate([upper_zero, upper_one], axis=0)[None]
    return (lower[None], upper, ancestor)


def solution(mesh):
    return jax.shard_map(
        local,
        mesh=mesh,
        in_specs=(
            P("gz", "row", "col"),
            P("gz", "row", "col"),
            P("gz", None, None, None),
            P("gz", None, None, None),
            P("gz", "row"),
        ),
        out_specs=(P("gz", "row", None), P("gz", None, "col"), P(("gz", "row"), "col")),
        check_vma=False,
    )
```

time: 469 us -> 265 us (0.57)
  waiting for transfers between devices: 308 us -> 129 us
  Pallas kernels: 0 us -> 61.7 us
  other arithmetic: 50.7 us -> 3.85 us
  local copies, waits for them, and re-layouts: 48.7 us -> 11.4 us
  matrix products: 30.5 us -> 0 us
  starting transfers between devices: 15.3 us -> 41.2 us
    psum x4 -> x0, waiting for transfers between devices: 236 us -> none  [from_root(): return lax.psum(block, axis)]
    pallas_call x0 -> x6, Pallas kernels: none -> 61.7 us  [the longest x1 21.4 us: local(): pl.pallas_call(pack_kernel, grid=(4,), in_specs=[whole((1, rows)), whole(...]
    ppermute x0 -> x19, waiting for transfers between devices: none -> 53.2 us  [the longest x12 30.4 us: tree(): block = block + lax.ppermute(block, axis, pairs)]
    dot_general x6 -> x0, matrix products: 30.5 us -> none  [the longest x2 16.4 us: update(): product = jnp.dot(lower_b, upper_b, preferred_element_type=jnp.float32)]
    scatter-add x1 -> x0, other arithmetic: 30.4 us -> none  [local(): ancestor = jnp.zeros((rows_local, col_width), jnp.float32).at[got_index.r...]
    ppermute x0 -> x19, starting transfers between devices: none -> 26.9 us  [the longest x12 21.6 us: tree(): block = block + lax.ppermute(block, axis, pairs)]
    scatter x2 -> x0, local copies, waits for them, and re-layouts: 22.3 us -> none  [the longest x1 14.3 us: local(): send_rows = jnp.zeros((peer_count * capacity, col_width), jnp.bfloat16).a...]
    another operation x2 -> x1, other arithmetic: 9.27 us -> 0.07 us  [local(): jnp.stack([lax.axis_index('row'), lax.axis_index('col')]).astype(jnp.int32)]
  transfers between devices with their start and end apart: 6 -> 22, of which waited for: 5 -> 9; matrix products, arithmetic and copies ran while one was open for 15% -> 1% of each run, Pallas kernels for 0% -> 14%
where the time goes in v1:
time: 265 us; the launch traced here: 262 us
  waiting for transfers between devices  129 us (49%)
  Pallas kernels  61.7 us (23%)
  starting transfers between devices  41.2 us (16%)
  between operations  14.5 us (5%)
  local copies, waits for them, and re-layouts  11.4 us (4%)
  other arithmetic  3.85 us (1%)
    all_to_all x1, waiting for transfers between devices, local(): lax.all_to_all(send.reshape(peers, CAP, width), ('gz', 'row'), split_axis...  75.5 us
    ppermute x12, waiting for transfers between devices, tree(): block = block + lax.ppermute(block, axis, pairs)  30.4 us
    ppermute x7, waiting for transfers between devices, spread(): piece = piece + lax.ppermute(lower[c * rows:(c + 1) * rows], axis, [(0, c)])  22.8 us
    ppermute x12, starting transfers between devices, tree(): block = block + lax.ppermute(block, axis, pairs)  21.6 us
    pallas_call x1, Pallas kernels, local(): pl.pallas_call(pack_kernel, grid=(4,), in_specs=[whole((1, rows)), whole(...  21.4 us
    pallas_call x1, Pallas kernels, local(): pl.pallas_call(add_kernel, grid=(8,), in_specs=[whole((1, slots)), whole(...  18.3 us
    pallas_call x1, Pallas kernels, local(): pl.pallas_call(update_kernel, grid=(4,), in_specs=[whole((1, rows)), whol...  13.3 us
    unnamed x26, local copies, waits for them, and re-layouts  8.86 us
  transfers between devices with their start and end apart: 22, of which 9 were waited for; matrix products, arithmetic and copies ran while one was open for 1% of the time, Pallas kernels for 14%

profile of v1, /device:TPU:96, one launch (start us, length us, event | category | flops | bytes accessed | tf_op | source)
XLA Modules:
  0.0 261.6 jit_solution(3057203472668117852)
XLA Ops:
  7.2 0.8 copy.11.pat_ref
  8.0 0.1 pad_add_fusion.pos_ref
  8.1 1.0 copy-done.3
  9.1 1.0 copy-done.5
  10.1 2.9 %panels_zero.1 = (bf16[2048,256]{1,0:T(8,128)(2,1)S(1)}, bf16[256,1024]{1,0:T(8,128)(2,1)S(1)}) custom-call(s32[2]{0:T(128)S(1)} %pad_add_fusion.pos_ref, s32[8,4]{1,0:T(8,128)S(1)} %copy.11.pat_ref, bf16[1,2048,1024]{2,1,0:T(8,128)(2,1)} %front_ref.1, bf16[1,2048,1024]{2,1,0:T(8,128)(2,1)} %front_ref.1, f32[1,2,256,256]{3,2,1,0:T(8,128)S(1)} %copy-done.3, ...), custom_call_target="tpu_custom_call" | custom-call | tf_op jit(solution)/shard_map/panels_zero/pallas_call | solution.py:166
  13.0 0.7 collective-permute-start.3
  13.7 4.9 %collective-permute-start = (bf16[256,256]{1,0:T(8,128)(2,1)S(1)}, bf16[256,256]{1,0:T(8,128)(2,1)S(1)}, u32[]{:S(2)}, u32[]{:S(2)}) collective-permute-start(bf16[256,256]{1,0:T(8,128)(2,1)S(1)} %slice_select_fusion.2), channel_id=1, source_target_pairs={{0,32},{1,33},{2,34},{3,35},{4,36},{5,37},{6,38},{7,39},{64,96},{6... | collective-permute-start | bytes 393224 | tf_op jit(solution)/shard_map/ppermute | solution.py:140
  18.7 0.8 collective-permute-start.4
  19.5 1.6 collective-permute-done
  21.2 1.3 collective-permute-start.1
  22.6 1.3 collective-permute-start.5
  23.9 1.1 collective-permute-done.1
  25.0 1.3 collective-permute-start.2
  26.3 0.1 constant_dynamic-update-slice_fusion.1
  26.4 9.8 %collective-permute-done.5 = bf16[256,256]{1,0:T(8,128)(2,1)S(1)} collective-permute-done((bf16[256,256]{1,0:T(8,128)(2,1)S(1)}, bf16[256,256]{1,0:T(8,128)(2,1)S(1)}, u32[]{:S(2)}, u32[]{:S(2)}) %collective-permute-start.5) | collective-permute-done | bytes 131104 | tf_op jit(solution)/shard_map/ppermute | solution.py:140
  36.3 4.3 %panels_one.1 = (bf16[2048,256]{1,0:T(8,128)(2,1)S(1)}, bf16[256,1024]{1,0:T(8,128)(2,1)S(1)}) custom-call(s32[2]{0:T(128)S(1)} %pad_add_fusion.pos_ref, s32[8,4]{1,0:T(8,128)S(1)} %copy.11.pat_ref, bf16[1,2048,1024]{2,1,0:T(8,128)(2,1)} %front_ref.1, bf16[1,2048,1024]{2,1,0:T(8,128)(2,1)} %front_ref.1, f32[1,2,256,256]{3,2,1,0:T(8,128)S(1)} %copy-done.4, ...), custom_call_target="tpu_custom_call" | custom-call | tf_op jit(solution)/shard_map/panels_one/pallas_call | solution.py:177
  40.7 0.1 constant_dynamic-update-slice_fusion
  40.7 0.2 fusion.7
  40.9 0.7 collective-permute-start.10
  41.6 0.7 collective-permute-start.11
  42.3 0.7 collective-permute-start.12
  43.0 0.7 collective-permute-start.6
  43.7 0.7 collective-permute-start.7
  44.4 1.3 collective-permute-start.8
  45.7 0.7 collective-permute-start.9
  46.4 22.8 %collective-permute-done.8 = bf16[256,512]{1,0:T(8,128)(2,1)S(1)} collective-permute-done((bf16[256,512]{1,0:T(8,128)(2,1)S(1)}, bf16[256,512]{1,0:T(8,128)(2,1)S(1)}, u32[]{:S(2)}, u32[]{:S(2)}) %collective-permute-start.8) | collective-permute-done | bytes 262176 | tf_op jit(solution)/shard_map/ppermute | solution.py:149
  69.2 0.8 fusion.6
  70.1 4.7 %collective-permute-start.13 = (bf16[256,1024]{1,0:T(8,128)(2,1)S(1)}, bf16[256,1024]{1,0:T(8,128)(2,1)S(1)}, u32[]{:S(2)}, u32[]{:S(2)}) collective-permute-start(bf16[256,1024]{1,0:T(8,128)(2,1)S(1)} %broadcast_select_fusion.1), channel_id=1, source_target_pairs={{0,32},{1,33},{2,34},{3,35},{4,36},{5,37},{6,38},{7,39},{64,96},{6... | collective-permute-start | bytes 1572872 | tf_op jit(solution)/shard_map/ppermute | solution.py:140
  74.8 1.3 collective-permute-start.16
  76.2 5.3 %collective-permute-done.13 = bf16[256,1024]{1,0:T(8,128)(2,1)S(1)} collective-permute-done((bf16[256,1024]{1,0:T(8,128)(2,1)S(1)}, bf16[256,1024]{1,0:T(8,128)(2,1)S(1)}, u32[]{:S(2)}, u32[]{:S(2)}) %collective-permute-start.13) | collective-permute-done | bytes 524320 | tf_op jit(solution)/shard_map/ppermute | solution.py:140
  81.4 0.1 fusion.8
  81.5 1.3 collective-permute-start.14
  82.8 4.2 %collective-permute-done.16 = bf16[256,1024]{1,0:T(8,128)(2,1)S(1)} collective-permute-done((bf16[256,1024]{1,0:T(8,128)(2,1)S(1)}, bf16[256,1024]{1,0:T(8,128)(2,1)S(1)}, u32[]{:S(2)}, u32[]{:S(2)}) %collective-permute-start.16) | collective-permute-done | bytes 524320 | tf_op jit(solution)/shard_map/ppermute | solution.py:140
  87.0 0.1 fusion.9
  87.1 1.3 collective-permute-start.17
  88.4 4.2 %collective-permute-done.14 = bf16[256,1024]{1,0:T(8,128)(2,1)S(1)} collective-permute-done((bf16[256,1024]{1,0:T(8,128)(2,1)S(1)}, bf16[256,1024]{1,0:T(8,128)(2,1)S(1)}, u32[]{:S(2)}, u32[]{:S(2)}) %collective-permute-start.14) | collective-permute-done | bytes 524320 | tf_op jit(solution)/shard_map/ppermute | solution.py:140
  92.7 0.2 add.84
  92.9 1.3 collective-permute-start.15
  94.2 4.1 %collective-permute-done.17 = bf16[256,1024]{1,0:T(8,128)(2,1)S(1)} collective-permute-done((bf16[256,1024]{1,0:T(8,128)(2,1)S(1)}, bf16[256,1024]{1,0:T(8,128)(2,1)S(1)}, u32[]{:S(2)}, u32[]{:S(2)}) %collective-permute-start.17) | collective-permute-done | bytes 524320 | tf_op jit(solution)/shard_map/ppermute | solution.py:140
  98.3 0.2 add.87
  98.5 1.3 collective-permute-start.18
  99.8 1.6 slots.1
  101.4 0.1 select_convert_fusion
  101.5 0.1 copy.13
  101.6 0.1 broadcast_in_dim.30
  101.7 0.1 pad.4.pat_ref
  101.8 2.2 copy-done
  104.0 0.8 copy-done.7
  104.9 0.7 copy-done.8
  105.6 21.4 %pack.1 = (bf16[3072,1024]{1,0:T(8,128)(2,1)}, bf16[3072,128]{1,0:T(8,128)(2,1)S(1)}, s32[8,3072]{1,0:T(8,128)S(1)}) custom-call(s32[1,2048]{1,0:T(1,128)S(1)} %copy-done.8, bf16[16,2048]{1,0:T(8,128)(2,1)S(1)} %copy-done.7, bf16[1,2048,1024]{2,1,0:T(8,128)(2,1)S(1)} %copy-done, bf16[2048,128]{1,0:T(8,128)(2,1)S(1)} %pad.4.pat_ref), custom_call_target="tpu_custom_call" | custom-call | tf_op jit(solution)/shard_map/pack/pallas_call | solution.py:197
  127.0 0.7 all_to_all.9
  127.6 6.9 %all-to-all-start = ((s32[32,1,96]{2,1,0:T(1,128)}), s32[32,1,96]{2,1,0:T(1,128)S(1)}, u32[]{:S(2)}, u32[]{:S(2)}) async-start(s32[32,1,96]{2,1,0:T(1,128)} %bitcast.6), calls=%async_computation | async-start | bytes 32768 | tf_op jit(solution)/shard_map/all_to_all | solution.py:214
  134.6 0.2 add.85.u0_ref
  134.8 0.2 add.88.u1_ref
  135.0 1.6 copy-done.1
  136.6 13.3 %update.1 = bf16[3072,1024]{1,0:T(8,128)(2,1)} custom-call(s32[1,2048]{1,0:T(1,128)S(1)} %copy-done.9, bf16[2048,512]{1,0:T(8,128)(2,1)S(1)} %copy-done.1, bf16[256,1024]{1,0:T(8,128)(2,1)S(1)} %add.85.u0_ref, bf16[256,1024]{1,0:T(8,128)(2,1)S(1)} %add.88.u1_ref, bf16[3072,1024]{1,0:T(8,128)(2,1)} %get-tuple-element.19.rows_ref, ...), custom_call_target="tpu_custom_call" | custom-call | tf_op jit(solution)/shard_map/update/pallas_call | solution.py:222
  149.9 7.3 %all-to-all-start.1 = ((bf16[32,96,1024]{2,1,0:T(8,128)(2,1)}), bf16[32,96,1024]{2,1,0:T(8,128)(2,1)}, u32[]{:S(2)}, u32[]{:S(2)}) async-start(bf16[32,96,1024]{2,1,0:T(8,128)(2,1)} %bitcast.12), calls=%async_computation.1 | async-start | bytes 12582912 | tf_op jit(solution)/shard_map/all_to_all | solution.py:238
  157.3 0.5 broadcast.33
  157.8 0.7 reduce.7
  158.5 0.1 reshape.28.index_ref
  158.6 1.0 maximum_bitcast_fusion
  159.6 75.5 %all-to-all-done.1 = bf16[32,96,1024]{2,1,0:T(8,128)(2,1)} async-done(((bf16[32,96,1024]{2,1,0:T(8,128)(2,1)}), bf16[32,96,1024]{2,1,0:T(8,128)(2,1)}, u32[]{:S(2)}, u32[]{:S(2)}) %all-to-all-start.1) | async-done | bytes 6291488 | tf_op jit(solution)/shard_map/all_to_all | solution.py:238
  235.2 18.3 %add.155 = f32[2048,1024]{1,0:T(8,128)} custom-call(s32[1,3072]{1,0:T(1,128)S(1)} %reshape.28.index_ref, bf16[3072,1024]{1,0:T(8,128)(2,1)} %bitcast.8.got_ref), custom_call_target="tpu_custom_call" | custom-call | tf_op jit(solution)/shard_map/add/pallas_call | solution.py:241
  253.4 1.3 copy.17
  (45 shorter events, 0.5 us)
Async XLA Ops:
  7.2 127.9 %all-gather.2.cloned.1.call-start = ((), (), s32[]{:S(2)}) async-start(), calls=%async_computation.2 | async-start | bytes 2359296 | tf_op jit(solution)/shard_map/all_gather | solution.py:150
  8.0 1.0 copy-start.3
  9.1 1.0 copy-start.5
  10.1 26.2 %copy-start.10 = (s32[2]{0:T(128)}, s32[2]{0:T(128)S(1)}, u32[]{:S(2)}) copy-start(s32[2]{0:T(128)S(1)} %pad_add_fusion.pos_ref) | copy-start | bytes 28
  13.0 5.7 %collective-permute-start.3 = (bf16[256,256]{1,0:T(8,128)(2,1)S(1)}, bf16[256,256]{1,0:T(8,128)(2,1)S(1)}, u32[]{:S(2)}, u32[]{:S(2)}) collective-permute-start(bf16[256,256]{1,0:T(8,128)(2,1)S(1)} %slice_select_fusion.1), channel_id=1, source_target_pairs={{0,4},{8,12},{16,20},{24,28},{32,36},{40,44},{48,52},{56,60},{64,6... | collective-permute-start | bytes 393224 | tf_op jit(solution)/shard_map/ppermute | solution.py:140
  13.7 7.4 %collective-permute-start = (bf16[256,256]{1,0:T(8,128)(2,1)S(1)}, bf16[256,256]{1,0:T(8,128)(2,1)S(1)}, u32[]{:S(2)}, u32[]{:S(2)}) collective-permute-start(bf16[256,256]{1,0:T(8,128)(2,1)S(1)} %slice_select_fusion.2), channel_id=1, source_target_pairs={{0,32},{1,33},{2,34},{3,35},{4,36},{5,37},{6,38},{7,39},{64,96},{6... | collective-permute-start | bytes 393224 | tf_op jit(solution)/shard_map/ppermute | solution.py:140
  18.7 17.6 %copy-start.4 = (f32[1,2,256,256]{3,2,1,0:T(8,128)S(1)}, f32[1,2,256,256]{3,2,1,0:T(8,128)}, u32[]{:S(2)}) copy-start(f32[1,2,256,256]{3,2,1,0:T(8,128)} %li_ref.3) | copy-start | bytes 1572868
  18.7 17.6 %copy-start.6 = (f32[1,2,256,256]{3,2,1,0:T(8,128)S(1)}, f32[1,2,256,256]{3,2,1,0:T(8,128)}, u32[]{:S(2)}) copy-start(f32[1,2,256,256]{3,2,1,0:T(8,128)} %ui_ref.3) | copy-start | bytes 1572868
  18.7 3.8 %collective-permute-start.4 = (bf16[256,256]{1,0:T(8,128)(2,1)S(1)}, bf16[256,256]{1,0:T(8,128)(2,1)S(1)}, u32[]{:S(2)}, u32[]{:S(2)}) collective-permute-start(bf16[256,256]{1,0:T(8,128)(2,1)S(1)} %fusion.10), channel_id=1, source_target_pairs={{0,2},{4,6},{8,10},{12,14},{16,18},{20,22},{24,26},{28,30},{32,34}... | collective-permute-start | bytes 393224 | tf_op jit(solution)/shard_map/ppermute | solution.py:140
  21.2 3.8 %collective-permute-start.1 = (bf16[256,256]{1,0:T(8,128)(2,1)S(1)}, bf16[256,256]{1,0:T(8,128)(2,1)S(1)}, u32[]{:S(2)}, u32[]{:S(2)}) collective-permute-start(bf16[256,256]{1,0:T(8,128)(2,1)S(1)} %fusion.11), channel_id=1, source_target_pairs={{0,16},{32,48},{1,17},{33,49},{2,18},{34,50},{3,19},{35,51},{4,20}... | collective-permute-start | bytes 393224 | tf_op jit(solution)/shard_map/ppermute | solution.py:140
  22.6 13.7 %collective-permute-start.5 = (bf16[256,256]{1,0:T(8,128)(2,1)S(1)}, bf16[256,256]{1,0:T(8,128)(2,1)S(1)}, u32[]{:S(2)}, u32[]{:S(2)}) collective-permute-start(bf16[256,256]{1,0:T(8,128)(2,1)S(1)} %add.74), channel_id=1, source_target_pairs={{0,1},{2,3},{4,5},{6,7},{8,9},{10,11},{12,13},{14,15},{16,17},{18,... | collective-permute-start | bytes 393224 | tf_op jit(solution)/shard_map/ppermute | solution.py:140
  25.0 11.2 %collective-permute-start.2 = (bf16[256,256]{1,0:T(8,128)(2,1)S(1)}, bf16[256,256]{1,0:T(8,128)(2,1)S(1)}, u32[]{:S(2)}, u32[]{:S(2)}) collective-permute-start(bf16[256,256]{1,0:T(8,128)(2,1)S(1)} %add.71), channel_id=1, source_target_pairs={{0,8},{16,24},{32,40},{48,56},{1,9},{17,25},{33,41},{49,57},{2,10}... | collective-permute-start | bytes 393224 | tf_op jit(solution)/shard_map/ppermute | solution.py:140
  40.9 3.4 %collective-permute-start.10 = (bf16[256,512]{1,0:T(8,128)(2,1)S(1)}, bf16[256,512]{1,0:T(8,128)(2,1)S(1)}, u32[]{:S(2)}, u32[]{:S(2)}) collective-permute-start(bf16[256,512]{1,0:T(8,128)(2,1)S(1)} %get-tuple-element.24), channel_id=1, source_target_pairs={{0,5},{8,13},{16,21},{24,29},{32,37},{40,45},{48,53},{56,61},{64,6... | collective-permute-start | bytes 786440 | tf_op jit(solution)/shard_map/ppermute | solution.py:149
  41.6 4.1 %collective-permute-start.11 = (bf16[256,512]{1,0:T(8,128)(2,1)S(1)}, bf16[256,512]{1,0:T(8,128)(2,1)S(1)}, u32[]{:S(2)}, u32[]{:S(2)}) collective-permute-start(bf16[256,512]{1,0:T(8,128)(2,1)S(1)} %get-tuple-element.23), channel_id=1, source_target_pairs={{0,6},{8,14},{16,22},{24,30},{32,38},{40,46},{48,54},{56,62},{64,7... | collective-permute-start | bytes 786440 | tf_op jit(solution)/shard_map/ppermute | solution.py:149
  42.3 4.1 %collective-permute-start.12 = (bf16[256,512]{1,0:T(8,128)(2,1)S(1)}, bf16[256,512]{1,0:T(8,128)(2,1)S(1)}, u32[]{:S(2)}, u32[]{:S(2)}) collective-permute-start(bf16[256,512]{1,0:T(8,128)(2,1)S(1)} %get-tuple-element.22), channel_id=1, source_target_pairs={{0,7},{8,15},{16,23},{24,31},{32,39},{40,47},{48,55},{56,63},{64,7... | collective-permute-start | bytes 786440 | tf_op jit(solution)/shard_map/ppermute | solution.py:149
  43.0 3.4 %collective-permute-start.6 = (bf16[256,512]{1,0:T(8,128)(2,1)S(1)}, bf16[256,512]{1,0:T(8,128)(2,1)S(1)}, u32[]{:S(2)}, u32[]{:S(2)}) collective-permute-start(bf16[256,512]{1,0:T(8,128)(2,1)S(1)} %get-tuple-element.21), channel_id=1, source_target_pairs={{0,1},{8,9},{16,17},{24,25},{32,33},{40,41},{48,49},{56,57},{64,65... | collective-permute-start | bytes 786440 | tf_op jit(solution)/shard_map/ppermute | solution.py:149
  43.7 2.7 %collective-permute-start.7 = (bf16[256,512]{1,0:T(8,128)(2,1)S(1)}, bf16[256,512]{1,0:T(8,128)(2,1)S(1)}, u32[]{:S(2)}, u32[]{:S(2)}) collective-permute-start(bf16[256,512]{1,0:T(8,128)(2,1)S(1)} %get-tuple-element.27), channel_id=1, source_target_pairs={{0,2},{8,10},{16,18},{24,26},{32,34},{40,42},{48,50},{56,58},{64,6... | collective-permute-start | bytes 786440 | tf_op jit(solution)/shard_map/ppermute | solution.py:149
  44.4 24.8 %collective-permute-start.8 = (bf16[256,512]{1,0:T(8,128)(2,1)S(1)}, bf16[256,512]{1,0:T(8,128)(2,1)S(1)}, u32[]{:S(2)}, u32[]{:S(2)}) collective-permute-start(bf16[256,512]{1,0:T(8,128)(2,1)S(1)} %get-tuple-element.26), channel_id=1, source_target_pairs={{0,3},{8,11},{16,19},{24,27},{32,35},{40,43},{48,51},{56,59},{64,6... | collective-permute-start | bytes 786440 | tf_op jit(solution)/shard_map/ppermute | solution.py:149
  45.7 23.5 %collective-permute-start.9 = (bf16[256,512]{1,0:T(8,128)(2,1)S(1)}, bf16[256,512]{1,0:T(8,128)(2,1)S(1)}, u32[]{:S(2)}, u32[]{:S(2)}) collective-permute-start(bf16[256,512]{1,0:T(8,128)(2,1)S(1)} %get-tuple-element.25), channel_id=1, source_target_pairs={{0,4},{8,12},{16,20},{24,28},{32,36},{40,44},{48,52},{56,60},{64,6... | collective-permute-start | bytes 786440 | tf_op jit(solution)/shard_map/ppermute | solution.py:149
  70.1 11.3 %collective-permute-start.13 = (bf16[256,1024]{1,0:T(8,128)(2,1)S(1)}, bf16[256,1024]{1,0:T(8,128)(2,1)S(1)}, u32[]{:S(2)}, u32[]{:S(2)}) collective-permute-start(bf16[256,1024]{1,0:T(8,128)(2,1)S(1)} %broadcast_select_fusion.1), channel_id=1, source_target_pairs={{0,32},{1,33},{2,34},{3,35},{4,36},{5,37},{6,38},{7,39},{64,96},{6... | collective-permute-start | bytes 1572872 | tf_op jit(solution)/shard_map/ppermute | solution.py:140
  74.8 12.2 %collective-permute-start.16 = (bf16[256,1024]{1,0:T(8,128)(2,1)S(1)}, bf16[256,1024]{1,0:T(8,128)(2,1)S(1)}, u32[]{:S(2)}, u32[]{:S(2)}) collective-permute-start(bf16[256,1024]{1,0:T(8,128)(2,1)S(1)} %broadcast_select_fusion), channel_id=1, source_target_pairs={{0,32},{1,33},{2,34},{3,35},{4,36},{5,37},{6,38},{7,39},{64,96},{6... | collective-permute-start | bytes 1572872 | tf_op jit(solution)/shard_map/ppermute | solution.py:140
  81.5 19.9 %copy-start.11 = (s32[1,8,4]{1,2,0:T(4,128)S(1)}, s32[1,8,4]{1,2,0:T(4,128)}, u32[]{:S(2)}) copy-start(s32[1,8,4]{1,2,0:T(4,128)} %param.6) | copy-start | bytes 388
  81.5 11.2 %collective-permute-start.14 = (bf16[256,1024]{1,0:T(8,128)(2,1)S(1)}, bf16[256,1024]{1,0:T(8,128)(2,1)S(1)}, u32[]{:S(2)}, u32[]{:S(2)}) collective-permute-start(bf16[256,1024]{1,0:T(8,128)(2,1)S(1)} %fusion.8), channel_id=1, source_target_pairs={{0,16},{32,48},{1,17},{33,49},{2,18},{34,50},{3,19},{35,51},{4,20}... | collective-permute-start | bytes 1572872 | tf_op jit(solution)/shard_map/ppermute | solution.py:140
  87.1 11.2 %collective-permute-start.17 = (bf16[256,1024]{1,0:T(8,128)(2,1)S(1)}, bf16[256,1024]{1,0:T(8,128)(2,1)S(1)}, u32[]{:S(2)}, u32[]{:S(2)}) collective-permute-start(bf16[256,1024]{1,0:T(8,128)(2,1)S(1)} %fusion.9), channel_id=1, source_target_pairs={{0,16},{32,48},{1,17},{33,49},{2,18},{34,50},{3,19},{35,51},{4,20}... | collective-permute-start | bytes 1572872 | tf_op jit(solution)/shard_map/ppermute | solution.py:140
  92.9 41.7 %collective-permute-start.15 = (bf16[256,1024]{1,0:T(8,128)(2,1)S(1)}, bf16[256,1024]{1,0:T(8,128)(2,1)S(1)}, u32[]{:S(2)}, u32[]{:S(2)}) collective-permute-start(bf16[256,1024]{1,0:T(8,128)(2,1)S(1)} %add.84), channel_id=1, source_target_pairs={{0,8},{16,24},{32,40},{48,56},{1,9},{17,25},{33,41},{49,57},{2,10}... | collective-permute-start | bytes 1572872 | tf_op jit(solution)/shard_map/ppermute | solution.py:140
  98.5 36.3 %collective-permute-start.18 = (bf16[256,1024]{1,0:T(8,128)(2,1)S(1)}, bf16[256,1024]{1,0:T(8,128)(2,1)S(1)}, u32[]{:S(2)}, u32[]{:S(2)}) collective-permute-start(bf16[256,1024]{1,0:T(8,128)(2,1)S(1)} %add.87), channel_id=1, source_target_pairs={{0,8},{16,24},{32,40},{48,56},{1,9},{17,25},{33,41},{49,57},{2,10}... | collective-permute-start | bytes 1572872 | tf_op jit(solution)/shard_map/ppermute | solution.py:140
  101.8 2.2 copy-start
  104.0 0.8 copy-start.7
  104.9 0.7 copy-start.8
  126.9 8.1 %copy-start.9 = (s32[1,2048]{1,0:T(1,128)S(1)}, s32[1,2048]{1,0:T(1,128)}, u32[]{:S(2)}) copy-start(s32[1,2048]{1,0:T(1,128)} %get-tuple-element.16.slot_ref) | copy-start | bytes 24580
  127.6 22.3 %all-to-all-start = ((s32[32,1,96]{2,1,0:T(1,128)}), s32[32,1,96]{2,1,0:T(1,128)S(1)}, u32[]{:S(2)}, u32[]{:S(2)}) async-start(s32[32,1,96]{2,1,0:T(1,128)} %bitcast.6), calls=%async_computation | async-start | bytes 32768 | tf_op jit(solution)/shard_map/all_to_all | solution.py:214
  135.0 1.6 copy-start.1
  149.9 85.2 %all-to-all-start.1 = ((bf16[32,96,1024]{2,1,0:T(8,128)(2,1)}), bf16[32,96,1024]{2,1,0:T(8,128)(2,1)}, u32[]{:S(2)}, u32[]{:S(2)}) async-start(bf16[32,96,1024]{2,1,0:T(8,128)(2,1)} %bitcast.12), calls=%async_computation.1 | async-start | bytes 12582912 | tf_op jit(solution)/shard_map/all_to_all | solution.py:238
  235.1 18.3 %copy-start.2 = (bf16[2048,512]{1,0:T(8,128)(2,1)S(1)}, bf16[2048,512]{1,0:T(8,128)(2,1)}, u32[]{:S(2)}) copy-start(bf16[2048,512]{1,0:T(8,128)(2,1)} %all-gather.2.cloned.1.call-done.lower_ref) | copy-start | bytes 6291460
Sparse Core Ops, SparseCore 0:
  70.2 44.8 all-gather.1

commit v2 on v1

v2 whole, which is shorter than its diff:
```python
import jax
import jax.numpy as jnp
from jax import lax
from jax.experimental import pallas as pl
from jax.experimental.pallas import tpu as pltpu
from jax.sharding import PartitionSpec as P

BF = jnp.bfloat16
F32 = jnp.float32
B = 256
CAP = 96
NOTE = 16
VMEM_LIMIT = 48 * 2**20


def params():
    return pltpu.CompilerParams(vmem_limit_bytes=VMEM_LIMIT)


def mm(a, b):
    return jnp.dot(a, b, preferred_element_type=F32)


def split(a):
    hi = a.astype(BF)
    return hi, (a - hi.astype(F32)).astype(BF)


def dot_split(a, b):
    ah, al = split(a)
    bh, bl = split(b)
    return mm(ah, bh) + (mm(ah, bl) + mm(al, bh))


def panels_zero_kernel(
    pos_ref, pat_ref, cols_ref, rows_ref, li_ref, ui_ref, send_ref, u_ref, corner_ref
):
    n_row, n_col = cols_ref.shape[1] // B, u_ref.shape[1] // B
    row0, col0 = pos_ref[0] * n_row, pos_ref[1] * n_col
    uh, ul = split(ui_ref[0, 0])
    lh, ll = split(li_ref[0, 0])
    for i in range(n_row):
        keep = jnp.where(row0 + i > 0, pat_ref[i, 0], 0).astype(F32)
        second = pat_ref[i, 1].astype(F32)
        block = cols_ref[0, i * B : (i + 1) * B, 0:B]
        base = i * (B + NOTE)
        send_ref[base : base + B, 0:B] = ((mm(block, uh) + mm(block, ul)) * keep).astype(BF)
        block = cols_ref[0, i * B : (i + 1) * B, B : 2 * B].astype(F32)
        send_ref[base : base + B, B : 2 * B] = (block * second).astype(BF)
        send_ref[base + B : base + B + NOTE, :] = (jnp.zeros((NOTE, 2 * B), F32) + second).astype(BF)
    for j in range(n_col):
        keep = jnp.where(col0 + j > 0, pat_ref[0, j], 0).astype(F32)
        block = rows_ref[0, 0:B, j * B : (j + 1) * B]
        u_ref[:, j * B : (j + 1) * B] = ((mm(lh, block) + mm(ll, block)) * keep).astype(BF)
    root = (pos_ref[1] == 0).astype(F32)
    corner_ref[0:B, :] = (send_ref[B + NOTE : 2 * B + NOTE, 0:B].astype(F32) * root).astype(BF)
    corner_ref[B : 2 * B, :] = (u_ref[:, B : 2 * B].astype(F32) * root).astype(BF)


def upper_kernel(pos_ref, pat_ref, rows_ref, li_ref, u0_ref, corner_ref, out_ref):
    n_col = u0_ref.shape[1] // B
    col0 = pos_ref[1] * n_col
    root = (pos_ref[0] == 0).astype(F32)
    out_ref[0:B, :] = (u0_ref[...].astype(F32) * root).astype(BF)
    n = B // n_col
    for j in range(n_col):
        keep = jnp.where(col0 + j > 1, pat_ref[1, j], 0).astype(F32)
        cols = slice(j * B, (j + 1) * B)
        block = rows_ref[0, B : 2 * B, cols].astype(F32) - mm(corner_ref[0:B, :], u0_ref[:, cols])
        out_ref[B : 2 * B, cols] = (dot_split(li_ref[0, 1], block) * (keep * root)).astype(BF)
        piece = corner_ref[B + j * n : B + (j + 1) * n, :].astype(F32)
        out_ref[2 * B : 2 * B + n, cols] = (piece * root).astype(BF)


def slots_kernel(pos_ref, targets_ref, slot_ref, value_ref):
    rows = targets_ref.shape[1]
    peers = 32
    target = targets_ref[...]
    peer = target // rows
    local = target - peer * rows
    row_id = pos_ref[0] * rows + lax.broadcasted_iota(jnp.int32, (1, rows), 1)
    valid = row_id >= 2 * B
    ids = lax.broadcasted_iota(jnp.int32, (peers, rows), 0)
    hot = jnp.where((ids == peer) & valid, 1.0, 0.0)
    before = jnp.where(
        lax.broadcasted_iota(jnp.int32, (B, B), 0) < lax.broadcasted_iota(jnp.int32, (B, B), 1), 1.0, 0.0
    ).astype(BF)
    seen = jnp.zeros((peers, 1), F32)
    for i in range(rows // B):
        part = hot[:, i * B : (i + 1) * B]
        rank = mm(part.astype(BF), before) + seen
        seen = seen + jnp.sum(part, axis=1, keepdims=True)
        place = rank + (CAP * ids[:, i * B : (i + 1) * B]).astype(F32)
        slot = jnp.sum(part * place, axis=0, keepdims=True).astype(jnp.int32)
        ok = valid[:, i * B : (i + 1) * B]
        slot_ref[:, i * B : (i + 1) * B] = jnp.where(ok, slot, -1)
    high = local // 64
    which = lax.broadcasted_iota(jnp.int32, (16, rows), 0)
    value = jnp.where(which == 0, high, jnp.where(which == 1, local - high * 64, jnp.where(which == 2, 1, 0)))
    value_ref[...] = value.astype(F32).astype(BF)


def one_hot(first, count, slot):
    ids = first + lax.broadcasted_iota(jnp.int32, (count, slot.shape[1]), 0)
    return jnp.where(ids == slot, 1.0, 0.0).astype(BF)


def pack_rows(first, hot, front_ref, keep, rows_ref):
    for j in range(rows_ref.shape[1] // B):
        cols = slice(j * B, (j + 1) * B)
        rows_ref[:, cols] = (mm(hot, front_ref[0, :, cols]) * keep[:, first + j : first + j + 1]).astype(BF)


def pack_head_kernel(first, slot_ref, value_ref, front_ref, pat_ref, *refs):
    rows_ref, keep_ref, index_ref = refs[-3:]
    count = rows_ref.shape[0]
    hot = one_hot((first + pl.program_id(0)) * count, count, slot_ref[...])
    keep = mm(hot, pat_ref[...])
    keep_ref[...] = keep.astype(BF)
    pack_rows(0, hot, front_ref, keep, rows_ref)
    info = lax.dot_general(value_ref[...], hot, (((1,), (1,)), ((), ())), preferred_element_type=F32)
    index = info[0:1] * 64.0 + info[1:2] + (1.0 - info[2:3]) * 4096.0
    index_ref[...] = jnp.broadcast_to(index, (8, count)).astype(jnp.int32)


def pack_tail_kernel(first, slot_ref, front_ref, keep_ref, after_ref, rows_ref):
    count = rows_ref.shape[0]
    hot = one_hot(pl.program_id(0) * count, count, slot_ref[...])
    pack_rows(first, hot, front_ref, keep_ref[...].astype(F32), rows_ref)


def subtract(out_ref, rows_ref, keep_ref, first, low, u_ref):
    for j in range(out_ref.shape[1] // B):
        cols = slice(j * B, (j + 1) * B)
        product = mm(low, u_ref[0 : 2 * B, cols])
        keep = keep_ref[:, first + j : first + j + 1].astype(F32)
        out_ref[:, cols] = (rows_ref[:, cols].astype(F32) - product * keep).astype(BF)


def update_kernel(
    pos_ref, slot_ref, all_ref, ui_ref, u_ref, rows_ref, keep_ref, out_ref, low_ref, lower_ref
):
    n_row = lower_ref.shape[0] // B
    n_col = u_ref.shape[1] // B

    @pl.when(pl.program_id(0) == 0)
    def _():
        corner = jnp.concatenate([u_ref[2 * B :, j * B : (j + 1) * B] for j in range(n_col)], axis=0)
        uh, ul = split(ui_ref[0, 1])
        for i in range(n_row):
            base, rows = i * (B + NOTE), slice(i * B, (i + 1) * B)
            low = all_ref[base : base + B, 0:B]
            keep = all_ref[base + B : base + B + NOTE, B : 2 * B].astype(F32)[0:1]
            keep = keep * (pos_ref[0] * n_row + i > 1).astype(F32)
            block = all_ref[base : base + B, B : 2 * B].astype(F32) - mm(low, corner)
            bh, bl = split(block)
            lower_ref[rows, 0:B] = low
            lower_ref[rows, B : 2 * B] = ((mm(bh, uh) + (mm(bh, ul) + mm(bl, uh))) * keep).astype(BF)

    count = rows_ref.shape[0]
    hot = one_hot(pl.program_id(0) * count, count, slot_ref[...])
    low = mm(hot, lower_ref[...]).astype(BF)
    low_ref[...] = low
    subtract(out_ref, rows_ref, keep_ref, 0, low, u_ref)


def rest_kernel(first, low_ref, u_ref, rows_ref, keep_ref, out_ref):
    subtract(out_ref, rows_ref, keep_ref, first, low_ref[...], u_ref)


def join_kernel(pos_ref, own_ref, *refs):
    piece_ref = refs[-1]
    piece = own_ref[...].astype(F32) * (pos_ref[1] == 0).astype(F32)
    for ref in refs[:-1]:
        piece = piece + ref[...].astype(F32)
    piece_ref[...] = piece.astype(BF)


def add_kernel(index_ref, got_ref, *refs):
    out_ref = refs[-1]
    hot = one_hot(pl.program_id(0) * out_ref.shape[0], out_ref.shape[0], index_ref[...])
    out_ref[...] = mm(hot, got_ref[...])


def cost(flops, size):
    return pl.CostEstimate(flops=flops, bytes_accessed=size, transcendentals=0)


def whole(shape):
    return pl.BlockSpec(shape, lambda *_: (0,) * len(shape))


SMEM = pl.BlockSpec(memory_space=pltpu.SMEM)
ANY = pl.BlockSpec(memory_space=pl.ANY)
TREE = (((0, 4),), ((0, 2), (4, 6)), ((0, 1), (2, 3), (4, 5), (6, 7)))


def tree(block, axis):
    for pairs in TREE:
        block = block + lax.ppermute(block, axis, pairs)
    return block


def sum_kernel(a_ref, b_ref, *refs):
    refs[-1][...] = (a_ref[...].astype(F32) + b_ref[...].astype(F32)).astype(BF)


def plus(a, b, *after):
    return pl.pallas_call(
        sum_kernel,
        grid=(1,),
        in_specs=[whole(a.shape)] * 2 + [ANY] * len(after),
        out_specs=whole(a.shape),
        out_shape=jax.ShapeDtypeStruct(a.shape, a.dtype),
        compiler_params=params(),
        cost_estimate=cost(0, 6 * a.size),
        name="plus",
    )(a, b, *after)


def scatter(lower, axis, pos):
    n = lax.axis_size(axis)
    rows = lower.shape[0] // n
    shape = (rows, lower.shape[1])
    got = [lax.ppermute(lower[c * rows : (c + 1) * rows], axis, [(0, c)]) for c in range(1, n)]
    return pl.pallas_call(
        join_kernel,
        grid=(1,),
        in_specs=[SMEM] + [whole(shape)] * n,
        out_specs=whole(shape),
        out_shape=jax.ShapeDtypeStruct(shape, lower.dtype),
        compiler_params=params(),
        cost_estimate=cost(0, 18 * rows * lower.shape[1]),
        name="join",
    )(pos, lower, *got)


def local(front_in, pattern, lower_inv, upper_inv, targets):
    rows, width = front_in.shape[1:]
    n_row, n_col = rows // B, width // B
    peers = lax.axis_size("gz") * lax.axis_size("row")
    slots = peers * CAP
    pos = jnp.stack([lax.axis_index("row"), lax.axis_index("col")]).astype(jnp.int32)
    pat = pattern[0]
    part = slots // 4
    head = 3 * width // 4
    tail = width - head
    last = head // tail
    exchange = lambda x: lax.all_to_all(x, ("gz", "row"), split_axis=0, concat_axis=0, tiled=True)

    slot, value = pl.pallas_call(
        slots_kernel,
        in_specs=[SMEM, pl.BlockSpec(memory_space=pltpu.VMEM)],
        out_shape=(jax.ShapeDtypeStruct((1, rows), jnp.int32), jax.ShapeDtypeStruct((16, rows), BF)),
        cost_estimate=cost(10**9, 10**6),
        name="slots",
    )(pos, targets)

    cols_spec = pl.BlockSpec((1, rows, 2 * B), lambda *_: (0, 0, 0))
    rows_spec = pl.BlockSpec((1, 2 * B, width), lambda *_: (0, 0, 0))
    inv_spec = whole((1, 2, B, B))
    sent = n_row * (B + NOTE)
    upper_rows = 2 * B + B // n_col
    send, u0, corner = pl.pallas_call(
        panels_zero_kernel,
        grid=(1,),
        in_specs=[SMEM, SMEM, cols_spec, rows_spec, inv_spec, inv_spec],
        out_specs=[whole((sent, 2 * B)), whole((B, width)), whole((2 * B, B))],
        out_shape=(
            jax.ShapeDtypeStruct((sent, 2 * B), BF),
            jax.ShapeDtypeStruct((B, width), BF),
            jax.ShapeDtypeStruct((2 * B, B), BF),
        ),
        compiler_params=params(),
        cost_estimate=cost(4 * (rows + width) * B * B, 8 * (rows + width) * B),
        name="panels_zero",
    )(pos, pat, front_in, front_in, lower_inv, upper_inv)
    piece = scatter(send, "col", pos)
    everything = lax.all_gather(piece, "col", axis=0, tiled=True)
    corner = tree(corner, "col")
    upper = pl.pallas_call(
        upper_kernel,
        grid=(1,),
        in_specs=[SMEM, SMEM, rows_spec, inv_spec, whole((B, width)), whole((2 * B, B))],
        out_specs=whole((upper_rows, width)),
        out_shape=jax.ShapeDtypeStruct((upper_rows, width), BF),
        compiler_params=params(),
        cost_estimate=cost(8 * width * B * B, 8 * width * B),
        name="upper",
    )(pos, pat, front_in, lower_inv, u0, corner)

    keep_col = (pos[1] * n_col + jnp.arange(n_col)) >= 2
    keep_pat = jnp.where(keep_col[None, :], pat, 0).astype(BF)
    pat_rows = jnp.pad(jnp.repeat(keep_pat, B, axis=0), ((0, 0), (0, 128 - n_col)))
    keep_spec = pl.BlockSpec((part, 128), lambda i: (i, 0))
    head_spec = pl.BlockSpec((part, head), lambda i: (i, 0))
    tail_spec = pl.BlockSpec((part, tail), lambda i: (i, 0))
    low_spec = pl.BlockSpec((part, 2 * B), lambda i: (i, 0))
    shapes = (
        jax.ShapeDtypeStruct((slots, head), BF),
        jax.ShapeDtypeStruct((slots, 128), BF),
        jax.ShapeDtypeStruct((8, slots), jnp.int32),
    )

    def pack_head(first, after, made):
        return pl.pallas_call(
            lambda *refs: pack_head_kernel(first, *refs),
            grid=(2,),
            in_specs=[
                whole((1, rows)),
                whole((16, rows)),
                pl.BlockSpec((1, rows, head), lambda i: (0, 0, 0)),
                whole((rows, 128)),
            ]
            + [ANY] * (1 + len(made)),
            out_specs=[
                pl.BlockSpec((part, head), lambda i: (first + i, 0)),
                pl.BlockSpec((part, 128), lambda i: (first + i, 0)),
                pl.BlockSpec((8, part), lambda i: (0, first + i)),
            ],
            out_shape=shapes,
            input_output_aliases={5 + i: i for i in range(len(made))},
            compiler_params=params(),
            cost_estimate=cost(4 * part * rows * (head + 512), 4 * (part + rows) * head),
            name="pack_head",
        )(slot, value, front_in, pat_rows, after, *made)

    made = pack_head(0, piece, ())
    upper = plus(upper, lax.ppermute(upper, "row", TREE[0]), made[1])
    made = pack_head(2, upper, made)
    packed_head, keep, index = made
    upper = plus(upper, lax.ppermute(upper, "row", TREE[1]), keep)
    upper = plus(upper, lax.ppermute(upper, "row", TREE[2]))
    got_index = exchange(index[0].reshape(peers, CAP)).reshape(1, slots)

    send_head, low, lower = pl.pallas_call(
        update_kernel,
        grid=(4,),
        in_specs=[
            SMEM,
            whole((1, rows)),
            whole((sent, 2 * B)),
            inv_spec,
            whole((upper_rows, width)),
            head_spec,
            keep_spec,
        ],
        out_specs=[head_spec, low_spec, whole((rows, 2 * B))],
        out_shape=(
            jax.ShapeDtypeStruct((slots, head), BF),
            jax.ShapeDtypeStruct((slots, 2 * B), BF),
            jax.ShapeDtypeStruct((rows, 2 * B), BF),
        ),
        compiler_params=params(),
        cost_estimate=cost(4 * slots * B * (rows + head), 4 * slots * head),
        name="update_head",
    )(pos, slot, everything, upper_inv, upper, packed_head, keep)
    got_head = exchange(send_head.reshape(peers, CAP, head)).reshape(slots, head)
    packed_tail = pl.pallas_call(
        lambda *refs: pack_tail_kernel(head // B, *refs),
        grid=(4,),
        in_specs=[
            whole((1, rows)),
            pl.BlockSpec((1, rows, tail), lambda i: (0, 0, last)),
            keep_spec,
            ANY,
        ],
        out_specs=tail_spec,
        out_shape=jax.ShapeDtypeStruct((slots, tail), BF),
        compiler_params=params(),
        cost_estimate=cost(2 * slots * rows * (tail + 256), 2 * (slots + rows) * tail),
        name="pack_tail",
    )(slot, front_in, keep, send_head)
    send_tail = pl.pallas_call(
        lambda *refs: rest_kernel(head // B, *refs),
        grid=(4,),
        in_specs=[low_spec, pl.BlockSpec((2 * B, tail), lambda i: (0, last)), tail_spec, keep_spec],
        out_specs=tail_spec,
        out_shape=jax.ShapeDtypeStruct((slots, tail), BF),
        compiler_params=params(),
        cost_estimate=cost(4 * slots * B * tail, 8 * slots * tail),
        name="update_tail",
    )(low, upper, packed_tail, keep)
    got_tail = exchange(send_tail.reshape(peers, CAP, tail)).reshape(slots, tail)

    ancestor = pl.pallas_call(
        add_kernel,
        grid=(8,),
        in_specs=[whole((1, slots)), whole((slots, head))],
        out_specs=pl.BlockSpec((rows // 8, head), lambda i: (i, 0)),
        out_shape=jax.ShapeDtypeStruct((rows, width), F32),
        compiler_params=params(),
        cost_estimate=cost(2 * rows * slots * head, 4 * (rows + slots) * head),
        name="add_head",
    )(got_index, got_head)
    ancestor = pl.pallas_call(
        add_kernel,
        grid=(8,),
        in_specs=[whole((1, slots)), whole((slots, tail)), ANY],
        out_specs=pl.BlockSpec((rows // 8, tail), lambda i: (i, last)),
        out_shape=jax.ShapeDtypeStruct((rows, width), F32),
        input_output_aliases={2: 0},
        compiler_params=params(),
        cost_estimate=cost(4 * rows * slots * tail, 4 * (rows + slots) * tail),
        name="add_tail",
    )(got_index, got_tail, ancestor)
    return (lower[None], upper[None, : 2 * B], ancestor)


def solution(mesh):
    return jax.shard_map(
        local,
        mesh=mesh,
        in_specs=(
            P("gz", "row", "col"),
            P("gz", "row", "col"),
            P("gz", None, None, None),
            P("gz", None, None, None),
            P("gz", "row"),
        ),
        out_specs=(P("gz", "row", None), P("gz", None, "col"), P(("gz", "row"), "col")),
        check_vma=False,
    )
```

time: 265 us -> 244 us (0.921)
  waiting for transfers between devices: 129 us -> 103 us
  Pallas kernels: 61.7 us -> 73.4 us
  starting transfers between devices: 41.2 us -> 34.6 us
  local copies, waits for them, and re-layouts: 11.4 us -> 16.2 us
  other arithmetic: 3.85 us -> 1.05 us
    ppermute x12 -> x3, starting transfers between devices: 21.6 us -> 2.78 us  [tree(): block = block + lax.ppermute(block, axis, pairs)]
    all_to_all x2 -> x3, waiting for transfers between devices: 75.5 us -> 57.1 us  [local(): lax.all_to_all(x, ('gz', 'row'), split_axis=0, concat_axis=0, tiled=True)]
    pallas_call x3 -> x10, Pallas kernels: 39 us -> 48.8 us  [the longest x2 20 us: pack_head(): pl.pallas_call(lambda *refs: pack_head_kernel(first, *refs), grid=(2,), i...]
    ppermute x12 -> x3, waiting for transfers between devices: 30.4 us -> 21.7 us  [tree(): block = block + lax.ppermute(block, axis, pairs)]
    ppermute x7 -> x10, starting transfers between devices: 5.36 us -> 13.2 us  [the longest x7 5.36 us: scatter(): lax.ppermute(lower[c * rows:(c + 1) * rows], axis, [(0, c)])]
    all_to_all x2 -> x3, starting transfers between devices: 14.2 us -> 18.6 us  [local(): lax.all_to_all(x, ('gz', 'row'), split_axis=0, concat_axis=0, tiled=True)]
    unnamed x26 -> x32, local copies, waits for them, and re-layouts: 8.86 us -> 11.9 us
    pallas_call x1 -> x2, Pallas kernels: 18.3 us -> 20.1 us  [local(): pl.pallas_call(add_kernel, grid=(8,), in_specs=[whole((1, slots)), whole(...]
  transfers between devices with their start and end apart: 22 -> 17, of which waited for: 9 -> 5; matrix products, arithmetic and copies ran while one was open for 1% -> 2% of each run, Pallas kernels for 14% -> 27%
where the time goes in v2:
time: 244 us; the launch traced here: 243 us
  waiting for transfers between devices  103 us (42%)
  Pallas kernels  73.4 us (30%)
  starting transfers between devices  34.6 us (14%)
  local copies, waits for them, and re-layouts  16.2 us (7%)
  between operations  14.4 us (6%)
    all_to_all x3, waiting for transfers between devices, local(): lax.all_to_all(x, ('gz', 'row'), split_axis=0, concat_axis=0, tiled=True)  57.1 us
    ppermute x3, waiting for transfers between devices, tree(): block = block + lax.ppermute(block, axis, pairs)  21.7 us
    ppermute x7, waiting for transfers between devices, scatter(): lax.ppermute(lower[c * rows:(c + 1) * rows], axis, [(0, c)])  21.7 us
    pallas_call x2, Pallas kernels, local(): pl.pallas_call(add_kernel, grid=(8,), in_specs=[whole((1, slots)), whole(...  20.1 us
    pallas_call x2, Pallas kernels, pack_head(): pl.pallas_call(lambda *refs: pack_head_kernel(first, *refs), grid=(2,), i...  20 us
    all_to_all x3, starting transfers between devices, local(): lax.all_to_all(x, ('gz', 'row'), split_axis=0, concat_axis=0, tiled=True)  18.6 us
    pallas_call x1, Pallas kernels, local(): pl.pallas_call(update_kernel, grid=(4,), in_specs=[SMEM, whole((1, rows))...  14.3 us
    unnamed x32, local copies, waits for them, and re-layouts  11.9 us
  transfers between devices with their start and end apart: 17, of which 5 were waited for; matrix products, arithmetic and copies ran while one was open for 2% of the time, Pallas kernels for 27%

profile of v2, /device:TPU:96, one launch (start us, length us, event | category | flops | bytes accessed | tf_op | source)
XLA Modules:
  0.0 243.1 jit_solution(17581463418360626230)
XLA Ops:
  7.2 0.0 all-gather.2.cloned.1.call-start
  7.2 0.8 copy.15.pat_ref
  8.0 0.1 pad_add_fusion.pos_ref
  8.1 1.0 copy-done.1
  9.1 1.0 copy-done.5
  10.1 2.9 %panels_zero.1 = (bf16[2176,512]{1,0:T(8,128)(2,1)S(1)}, bf16[256,1024]{1,0:T(8,128)(2,1)S(1)}, bf16[512,256]{1,0:T(8,128)(2,1)S(1)}) custom-call(s32[2]{0:T(128)S(1)} %pad_add_fusion.pos_ref, s32[8,4]{1,0:T(8,128)S(1)} %copy.15.pat_ref, bf16[1,2048,1024]{2,1,0:T(8,128)(2,1)} %refs_1_.1, bf16[1,2048,1024]{2,1,0:T(8,128)(2,1)} %refs_1_.1, ...), custom_call_target="tpu_custom_call" | custom-call | flops 805306368 | bytes 6291456 | tf_op jit(solution)/shard_map/panels_zero/pallas_call | solution.py:264
  13.1 0.1 fusion
  13.2 0.7 collective-permute-start.6
  13.9 0.7 collective-permute-start.5
  14.6 0.7 collective-permute-start.7
  15.3 0.7 collective-permute-start.4
  16.0 0.7 collective-permute-start.3
  16.7 1.3 collective-permute-start.2
  18.0 0.7 collective-permute-start.1
  18.7 0.7 collective-permute-start
  19.4 0.1 add.21
  19.4 0.0 copy-start.2
  19.4 0.8 collective-permute-start.8
  20.3 21.7 %collective-permute-done.2.refs_2_ = bf16[272,512]{1,0:T(8,128)(2,1)S(1)} collective-permute-done((bf16[272,512]{1,0:T(8,128)(2,1)S(1)}, bf16[272,512]{1,0:T(8,128)(2,1)S(1)}, u32[]{:S(2)}, u32[]{:S(2)}) %collective-permute-start.2) | collective-permute-done | bytes 278560 | tf_op jit(solution)/shard_map/ppermute | solution.py:225
  42.0 1.6 join.1.refs_4_
  43.6 0.0 all-gather.2.cloned.1.call-update
  43.6 0.1 add.22
  43.7 1.3 collective-permute-start.9
  45.0 21.7 %collective-permute-done.9 = bf16[512,256]{1,0:T(8,128)(2,1)S(1)} collective-permute-done((bf16[512,256]{1,0:T(8,128)(2,1)S(1)}, bf16[512,256]{1,0:T(8,128)(2,1)S(1)}, u32[]{:S(2)}, u32[]{:S(2)}) %collective-permute-start.9) | collective-permute-done | bytes 262176 | tf_op jit(solution)/shard_map/ppermute | solution.py:200
  66.7 0.1 add.23.corner_ref
  66.8 2.3 upper.1.a_ref
  69.1 5.1 %collective-permute-start.10 = (bf16[576,1024]{1,0:T(8,128)(2,1)S(1)}, bf16[576,1024]{1,0:T(8,128)(2,1)S(1)}, u32[]{:S(2)}, u32[]{:S(2)}) collective-permute-start(bf16[576,1024]{1,0:T(8,128)(2,1)S(1)} %upper.1.a_ref), channel_id=1, source_target_pairs={{0,32},{1,33},{2,34},{3,35},{4,36},{5,37},{6,38},{7,39},{64,96},{6... | collective-permute-start | bytes 3538952 | tf_op jit(solution)/shard_map/ppermute | solution.py:329
  74.3 0.1 select_convert_fusion
  74.4 0.1 copy.17
  74.5 0.1 broadcast_in_dim.24
  74.5 0.9 pad.4.refs_3_
  75.4 1.6 slots.1
  77.0 2.2 copy-done
  79.3 1.0 copy-done.7
  80.3 0.8 copy-done.12
  81.2 0.7 copy-done.13
  81.9 9.1 %pack_head.2 = (bf16[3072,768]{1,0:T(8,128)(2,1)}, bf16[3072,128]{1,0:T(8,128)(2,1)S(1)}, s32[8,3072]{1,0:T(8,128)S(1)}) custom-call(s32[1,2048]{1,0:T(1,128)S(1)} %copy-done.13, bf16[16,2048]{1,0:T(8,128)(2,1)S(1)} %copy-done.12, bf16[1,2048,1024]{2,1,0:T(8,128)(2,1)S(1)} %copy-done, bf16[2048,128]{1,0:T(8,128)(2,1)S(1)} %copy-done.7, ...), custom_call_target="tpu_custom_call" | custom-call | flops 8053063680 | bytes 8650752 | tf_op jit(solution)/shard_map/pack_head/pallas_call | solution.py:306
  91.0 0.3 plus.3.refs_4_.a_ref
  91.2 1.4 collective-permute-start.11
  92.6 10.8 %pack_head.3 = (bf16[3072,768]{1,0:T(8,128)(2,1)}, bf16[3072,128]{1,0:T(8,128)(2,1)S(1)}, s32[8,3072]{1,0:T(8,128)S(1)}) custom-call(s32[1,2048]{1,0:T(1,128)S(1)} %copy-done.13, bf16[16,2048]{1,0:T(8,128)(2,1)S(1)} %copy-done.12, bf16[1,2048,1024]{2,1,0:T(8,128)(2,1)} %refs_1_.1, ...), custom_call_target="tpu_custom_call", output_to_operand_aliasing={{0}: (5, {}), {1}: (6, {}), {2}: (7, {})} | custom-call | flops 8053063680 | bytes 8650752 | tf_op jit(solution)/shard_map/pack_head/pallas_call | solution.py:306
  103.5 2.8 %collective-permute-done.11.b_ref = bf16[576,1024]{1,0:T(8,128)(2,1)S(1)} collective-permute-done((bf16[576,1024]{1,0:T(8,128)(2,1)S(1)}, bf16[576,1024]{1,0:T(8,128)(2,1)S(1)}, u32[]{:S(2)}, u32[]{:S(2)}) %collective-permute-start.11) | collective-permute-done | bytes 1179680 | tf_op jit(solution)/shard_map/ppermute | solution.py:332
  106.3 0.3 plus.4.a_ref
  106.5 1.4 collective-permute-start.12
  108.0 0.7 all_to_all.12
  108.6 7.3 %all-to-all-start = ((s32[32,1,96]{2,1,0:T(1,128)}), s32[32,1,96]{2,1,0:T(1,128)S(1)}, u32[]{:S(2)}, u32[]{:S(2)}) async-start(s32[32,1,96]{2,1,0:T(1,128)} %bitcast.6), calls=%async_computation | async-start | bytes 32768 | tf_op jit(solution)/shard_map/all_to_all | solution.py:249
  116.0 1.0 copy-done.3
  117.0 1.3 copy-done.4
  118.2 0.3 plus.5.u_ref.refs_1_
  118.5 0.0 all-gather.2.cloned.1.call-done.all_ref
  118.6 1.0 copy-done.6
  119.6 1.6 copy-done.11
  121.2 14.3 %update_head.1 = (bf16[3072,768]{1,0:T(8,128)(2,1)}, bf16[3072,512]{1,0:T(8,128)(2,1)}, bf16[2048,512]{1,0:T(8,128)(2,1)}) custom-call(s32[2]{0:T(128)S(1)} %copy-done.10, s32[1,2048]{1,0:T(1,128)S(1)} %copy-done.14, bf16[2176,512]{1,0:T(8,128)(2,1)S(1)} %copy-done.11, f32[1,2,256,256]{3,2,1,0:T(8,128)S(1)} %copy-done.6, ...), custom_call_target="tpu_custom_call" | custom-call | flops 8858370048 | bytes 9437184 | tf_op jit(solution)/shard_map/update_head/pallas_call | solution.py:336
  135.5 7.3 %all-to-all-start.2 = ((bf16[32,96,768]{2,1,0:T(8,128)(2,1)}), bf16[32,96,768]{2,1,0:T(8,128)(2,1)}, u32[]{:S(2)}, u32[]{:S(2)}) async-start(bf16[32,96,768]{2,1,0:T(8,128)(2,1)} %bitcast.14), calls=%async_computation.2 | async-start | bytes 9437184 | tf_op jit(solution)/shard_map/all_to_all | solution.py:249
  142.9 5.2 %pack_tail.1.refs_2_ = bf16[3072,256]{1,0:T(8,128)(2,1)S(1)} custom-call(s32[1,2048]{1,0:T(1,128)S(1)} %copy-done.14, bf16[1,2048,1024]{2,1,0:T(8,128)(2,1)} %refs_1_.1, bf16[3072,128]{1,0:T(8,128)(2,1)S(1)} %get-tuple-element.25.refs_0_.keep_ref.refs_2_.refs_3_, bf16[3072,768]{1,0:T(8,128)(2,1)} %get-tuple-element.30.refs_3_), custom_call_target="tpu_custom_call" | custom-call | flops 6442450944 | bytes 2621440 | tf_op jit(solution)/shard_map/pack_tail/pallas_call | solution.py:359
  148.1 4.6 %update_tail.1 = bf16[3072,256]{1,0:T(8,128)(2,1)} custom-call(bf16[3072,512]{1,0:T(8,128)(2,1)} %get-tuple-element.29.refs_0_, bf16[576,1024]{1,0:T(8,128)(2,1)S(1)} %plus.5.u_ref.refs_1_, bf16[3072,256]{1,0:T(8,128)(2,1)S(1)} %pack_tail.1.refs_2_, bf16[3072,128]{1,0:T(8,128)(2,1)S(1)} %get-tuple-element.25.refs_0_.keep_ref.refs_2_.refs_3_), custom_call_target="tpu_custom_call" | custom-call | flops 805306368 | bytes 6291456 | tf_op jit(solution)/shard_map/update_tail/pallas_call | solution.py:374
  152.7 49.9 %all-to-all-done.2 = bf16[32,96,768]{2,1,0:T(8,128)(2,1)} async-done(((bf16[32,96,768]{2,1,0:T(8,128)(2,1)}), bf16[32,96,768]{2,1,0:T(8,128)(2,1)}, u32[]{:S(2)}, u32[]{:S(2)}) %all-to-all-start.2) | async-done | bytes 4718624 | tf_op jit(solution)/shard_map/all_to_all | solution.py:249
  202.6 4.0 %all-to-all-start.1 = ((bf16[32,96,256]{2,1,0:T(8,128)(2,1)}), bf16[32,96,256]{2,1,0:T(8,128)(2,1)S(1)}, u32[]{:S(2)}, u32[]{:S(2)}) async-start(bf16[32,96,256]{2,1,0:T(8,128)(2,1)} %bitcast.7), calls=%async_computation.1 | async-start | bytes 3145728 | tf_op jit(solution)/shard_map/all_to_all | solution.py:249
  206.6 0.5 broadcast.21
  207.1 0.7 reduce.7
  207.8 0.1 reshape.34.index_ref
  207.9 1.0 slice_bitcast_fusion
  208.9 14.4 %add_head.1.refs_0_ = f32[2048,1024]{1,0:T(8,128)} custom-call(s32[1,3072]{1,0:T(1,128)S(1)} %reshape.34.index_ref, bf16[3072,768]{1,0:T(8,128)(2,1)} %bitcast.10.got_ref), custom_call_target="tpu_custom_call" | custom-call | flops 9663676416 | bytes 15728640 | tf_op jit(solution)/shard_map/add_head/pallas_call | solution.py:386
  223.3 7.2 %all-to-all-done.1 = bf16[32,96,256]{2,1,0:T(8,128)(2,1)S(1)} async-done(((bf16[32,96,256]{2,1,0:T(8,128)(2,1)}), bf16[32,96,256]{2,1,0:T(8,128)(2,1)S(1)}, u32[]{:S(2)}, u32[]{:S(2)}) %all-to-all-start.1) | async-done | bytes 1572896 | tf_op jit(solution)/shard_map/all_to_all | solution.py:249
  230.5 5.7 %add_tail.1 = f32[2048,1024]{1,0:T(8,128)} custom-call(s32[1,3072]{1,0:T(1,128)S(1)} %reshape.34.index_ref, bf16[3072,256]{1,0:T(8,128)(2,1)S(1)} %bitcast.13, f32[2048,1024]{1,0:T(8,128)} %add_head.1.refs_0_), custom_call_target="tpu_custom_call", output_to_operand_aliasing={{}: (2, {})} | custom-call | flops 6442450944 | bytes 5242880 | tf_op jit(solution)/shard_map/add_tail/pallas_call | solution.py:396
  (34 shorter events, 0.1 us)
Async XLA Ops:
  7.2 111.4 %all-gather.2.cloned.1.call-start = ((), (), s32[]{:S(2)}) async-start(), calls=%async_computation.3 | async-start | bytes 2506752 | tf_op jit(solution)/shard_map/all_gather | solution.py:279
  8.0 1.0 copy-start.1
  9.1 1.0 copy-start.5
  10.1 56.6 %copy-start.9 = (s32[2]{0:T(128)}, s32[2]{0:T(128)S(1)}, u32[]{:S(2)}) copy-start(s32[2]{0:T(128)S(1)} %pad_add_fusion.pos_ref) | copy-start | bytes 28
  13.2 4.7 %collective-permute-start.6 = (bf16[272,512]{1,0:T(8,128)(2,1)S(1)}, bf16[272,512]{1,0:T(8,128)(2,1)S(1)}, u32[]{:S(2)}, u32[]{:S(2)}) collective-permute-start(bf16[272,512]{1,0:T(8,128)(2,1)S(1)} %get-tuple-element.31), channel_id=1, source_target_pairs={{0,7},{8,15},{16,23},{24,31},{32,39},{40,47},{48,55},{56,63},{64,7... | collective-permute-start | bytes 835592 | tf_op jit(solution)/shard_map/ppermute | solution.py:225
  13.9 4.8 %collective-permute-start.5 = (bf16[272,512]{1,0:T(8,128)(2,1)S(1)}, bf16[272,512]{1,0:T(8,128)(2,1)S(1)}, u32[]{:S(2)}, u32[]{:S(2)}) collective-permute-start(bf16[272,512]{1,0:T(8,128)(2,1)S(1)} %get-tuple-element.32), channel_id=1, source_target_pairs={{0,6},{8,14},{16,22},{24,30},{32,38},{40,46},{48,54},{56,62},{64,7... | collective-permute-start | bytes 835592 | tf_op jit(solution)/shard_map/ppermute | solution.py:225
  14.6 2.1 collective-permute-start.7
  15.3 4.2 %collective-permute-start.4 = (bf16[272,512]{1,0:T(8,128)(2,1)S(1)}, bf16[272,512]{1,0:T(8,128)(2,1)S(1)}, u32[]{:S(2)}, u32[]{:S(2)}) collective-permute-start(bf16[272,512]{1,0:T(8,128)(2,1)S(1)} %get-tuple-element.33), channel_id=1, source_target_pairs={{0,5},{8,13},{16,21},{24,29},{32,37},{40,45},{48,53},{56,61},{64,6... | collective-permute-start | bytes 835592 | tf_op jit(solution)/shard_map/ppermute | solution.py:225
  16.0 4.3 %collective-permute-start.3 = (bf16[272,512]{1,0:T(8,128)(2,1)S(1)}, bf16[272,512]{1,0:T(8,128)(2,1)S(1)}, u32[]{:S(2)}, u32[]{:S(2)}) collective-permute-start(bf16[272,512]{1,0:T(8,128)(2,1)S(1)} %get-tuple-element.34), channel_id=1, source_target_pairs={{0,4},{8,12},{16,20},{24,28},{32,36},{40,44},{48,52},{56,60},{64,6... | collective-permute-start | bytes 835592 | tf_op jit(solution)/shard_map/ppermute | solution.py:225
  16.7 25.3 %collective-permute-start.2 = (bf16[272,512]{1,0:T(8,128)(2,1)S(1)}, bf16[272,512]{1,0:T(8,128)(2,1)S(1)}, u32[]{:S(2)}, u32[]{:S(2)}) collective-permute-start(bf16[272,512]{1,0:T(8,128)(2,1)S(1)} %get-tuple-element.35), channel_id=1, source_target_pairs={{0,3},{8,11},{16,19},{24,27},{32,35},{40,43},{48,51},{56,59},{64,6... | collective-permute-start | bytes 835592 | tf_op jit(solution)/shard_map/ppermute | solution.py:225
  18.0 24.0 %collective-permute-start.1 = (bf16[272,512]{1,0:T(8,128)(2,1)S(1)}, bf16[272,512]{1,0:T(8,128)(2,1)S(1)}, u32[]{:S(2)}, u32[]{:S(2)}) collective-permute-start(bf16[272,512]{1,0:T(8,128)(2,1)S(1)} %get-tuple-element.36), channel_id=1, source_target_pairs={{0,2},{8,10},{16,18},{24,26},{32,34},{40,42},{48,50},{56,58},{64,6... | collective-permute-start | bytes 835592 | tf_op jit(solution)/shard_map/ppermute | solution.py:225
  18.7 23.3 %collective-permute-start = (bf16[272,512]{1,0:T(8,128)(2,1)S(1)}, bf16[272,512]{1,0:T(8,128)(2,1)S(1)}, u32[]{:S(2)}, u32[]{:S(2)}) collective-permute-start(bf16[272,512]{1,0:T(8,128)(2,1)S(1)} %get-tuple-element.37), channel_id=1, source_target_pairs={{0,1},{8,9},{16,17},{24,25},{32,33},{40,41},{48,49},{56,57},{64,65... | collective-permute-start | bytes 835592 | tf_op jit(solution)/shard_map/ppermute | solution.py:225
  19.4 47.3 %copy-start.2 = (f32[1,2,256,256]{3,2,1,0:T(8,128)S(1)}, f32[1,2,256,256]{3,2,1,0:T(8,128)}, u32[]{:S(2)}) copy-start(f32[1,2,256,256]{3,2,1,0:T(8,128)} %li_ref.3) | copy-start | bytes 1572868
  19.4 24.1 %collective-permute-start.8 = (bf16[512,256]{1,0:T(8,128)(2,1)S(1)}, bf16[512,256]{1,0:T(8,128)(2,1)S(1)}, u32[]{:S(2)}, u32[]{:S(2)}) collective-permute-start(bf16[512,256]{1,0:T(8,128)(2,1)S(1)} %add.21), channel_id=1, source_target_pairs={{0,2},{4,6},{8,10},{12,14},{16,18},{20,22},{24,26},{28,30},{32,34}... | collective-permute-start | bytes 786440 | tf_op jit(solution)/shard_map/ppermute | solution.py:200
  43.7 23.0 %collective-permute-start.9 = (bf16[512,256]{1,0:T(8,128)(2,1)S(1)}, bf16[512,256]{1,0:T(8,128)(2,1)S(1)}, u32[]{:S(2)}, u32[]{:S(2)}) collective-permute-start(bf16[512,256]{1,0:T(8,128)(2,1)S(1)} %add.22), channel_id=1, source_target_pairs={{0,1},{2,3},{4,5},{6,7},{8,9},{10,11},{12,13},{14,15},{16,17},{18,... | collective-permute-start | bytes 786440 | tf_op jit(solution)/shard_map/ppermute | solution.py:200
  66.8 7.5 %copy-start.15 = (s32[1,8,4]{1,2,0:T(4,128)S(1)}, s32[1,8,4]{1,2,0:T(4,128)}, u32[]{:S(2)}) copy-start(s32[1,8,4]{1,2,0:T(4,128)} %param.6) | copy-start | bytes 388
  69.1 21.8 %collective-permute-start.10 = (bf16[576,1024]{1,0:T(8,128)(2,1)S(1)}, bf16[576,1024]{1,0:T(8,128)(2,1)S(1)}, u32[]{:S(2)}, u32[]{:S(2)}) collective-permute-start(bf16[576,1024]{1,0:T(8,128)(2,1)S(1)} %upper.1.a_ref), channel_id=1, source_target_pairs={{0,32},{1,33},{2,34},{3,35},{4,36},{5,37},{6,38},{7,39},{64,96},{6... | collective-permute-start | bytes 3538952 | tf_op jit(solution)/shard_map/ppermute | solution.py:329
  77.0 2.2 copy-start
  79.3 1.0 copy-start.7
  80.3 0.8 copy-start.12
  81.2 0.7 copy-start.13
  91.0 1.6 copy-start.8
  91.2 15.0 %collective-permute-start.11 = (bf16[576,1024]{1,0:T(8,128)(2,1)S(1)}, bf16[576,1024]{1,0:T(8,128)(2,1)S(1)}, u32[]{:S(2)}, u32[]{:S(2)}) collective-permute-start(bf16[576,1024]{1,0:T(8,128)(2,1)S(1)} %plus.3.refs_4_.a_ref), channel_id=1, source_target_pairs={{0,16},{32,48},{1,17},{33,49},{2,18},{34,50},{3,19},{35,51},{4,20}... | collective-permute-start | bytes 3538952 | tf_op jit(solution)/shard_map/ppermute | solution.py:332
  106.5 12.0 %copy-start.10 = (s32[2]{0:T(128)S(1)}, s32[2]{0:T(128)}, u32[]{:S(2)}) copy-start(s32[2]{0:T(128)} %copy-done.9) | copy-start | bytes 28
  106.5 12.0 %copy-start.14 = (s32[1,2048]{1,0:T(1,128)S(1)}, s32[1,2048]{1,0:T(1,128)}, u32[]{:S(2)}) copy-start(s32[1,2048]{1,0:T(1,128)} %get-tuple-element.17.refs_0_.slot_ref) | copy-start | bytes 24580
  106.5 9.4 %collective-permute-start.12 = (bf16[576,1024]{1,0:T(8,128)(2,1)S(1)}, bf16[576,1024]{1,0:T(8,128)(2,1)S(1)}, u32[]{:S(2)}, u32[]{:S(2)}) collective-permute-start(bf16[576,1024]{1,0:T(8,128)(2,1)S(1)} %plus.4.a_ref), channel_id=1, source_target_pairs={{0,8},{16,24},{32,40},{48,56},{1,9},{17,25},{33,41},{49,57},{2,10}... | collective-permute-start | bytes 3538952 | tf_op jit(solution)/shard_map/ppermute | solution.py:333
  108.6 26.9 %all-to-all-start = ((s32[32,1,96]{2,1,0:T(1,128)}), s32[32,1,96]{2,1,0:T(1,128)S(1)}, u32[]{:S(2)}, u32[]{:S(2)}) async-start(s32[32,1,96]{2,1,0:T(1,128)} %bitcast.6), calls=%async_computation | async-start | bytes 32768 | tf_op jit(solution)/shard_map/all_to_all | solution.py:249
  116.0 1.0 copy-start.3
  117.0 1.3 copy-start.4
  118.6 1.0 copy-start.6
  119.6 1.6 copy-start.11
  135.5 67.1 %all-to-all-start.2 = ((bf16[32,96,768]{2,1,0:T(8,128)(2,1)}), bf16[32,96,768]{2,1,0:T(8,128)(2,1)}, u32[]{:S(2)}, u32[]{:S(2)}) async-start(bf16[32,96,768]{2,1,0:T(8,128)(2,1)} %bitcast.14), calls=%async_computation.2 | async-start | bytes 9437184 | tf_op jit(solution)/shard_map/all_to_all | solution.py:249
  202.6 27.9 %all-to-all-start.1 = ((bf16[32,96,256]{2,1,0:T(8,128)(2,1)}), bf16[32,96,256]{2,1,0:T(8,128)(2,1)S(1)}, u32[]{:S(2)}, u32[]{:S(2)}) async-start(bf16[32,96,256]{2,1,0:T(8,128)(2,1)} %bitcast.7), calls=%async_computation.1 | async-start | bytes 3145728 | tf_op jit(solution)/shard_map/all_to_all | solution.py:249
Sparse Core Ops, SparseCore 0:
  43.7 50.0 all-gather.1

commit v3 on v2

--- a/solution.py
+++ b/solution.py
@@ -168,10 +168,10 @@
     subtract(out_ref, rows_ref, keep_ref, first, low_ref[...], u_ref)
 
 
-def join_kernel(pos_ref, own_ref, *refs):
+def join_kernel(count, pos_ref, own_ref, *refs):
     piece_ref = refs[-1]
     piece = own_ref[...].astype(F32) * (pos_ref[1] == 0).astype(F32)
-    for ref in refs[:-1]:
+    for ref in refs[:count]:
         piece = piece + ref[...].astype(F32)
     piece_ref[...] = piece.astype(BF)
 
@@ -218,21 +218,21 @@
     )(a, b, *after)
 
 
-def scatter(lower, axis, pos):
+def scatter(lower, axis, pos, *after):
     n = lax.axis_size(axis)
     rows = lower.shape[0] // n
     shape = (rows, lower.shape[1])
     got = [lax.ppermute(lower[c * rows : (c + 1) * rows], axis, [(0, c)]) for c in range(1, n)]
     return pl.pallas_call(
-        join_kernel,
+        lambda *refs: join_kernel(n - 1, *refs),
         grid=(1,),
-        in_specs=[SMEM] + [whole(shape)] * n,
+        in_specs=[SMEM] + [whole(shape)] * n + [ANY] * len(after),
         out_specs=whole(shape),
         out_shape=jax.ShapeDtypeStruct(shape, lower.dtype),
         compiler_params=params(),
         cost_estimate=cost(0, 18 * rows * lower.shape[1]),
         name="join",
-    )(pos, lower, *got)
+    )(pos, lower, *got, *after)
 
 
 def local(front_in, pattern, lower_inv, upper_inv, targets):
@@ -275,7 +275,10 @@
         cost_estimate=cost(4 * (rows + width) * B * B, 8 * (rows + width) * B),
         name="panels_zero",
     )(pos, pat, front_in, front_in, lower_inv, upper_inv)
-    piece = scatter(send, "col", pos)
+    keep_col = (pos[1] * n_col + jnp.arange(n_col)) >= 2
+    keep_pat = jnp.where(keep_col[None, :], pat, 0).astype(BF)
+    pat_rows = jnp.pad(jnp.repeat(keep_pat, B, axis=0), ((0, 0), (0, 128 - n_col)))
+    piece = scatter(send, "col", pos, slot, value, pat_rows)
     everything = lax.all_gather(piece, "col", axis=0, tiled=True)
     corner = tree(corner, "col")
     upper = pl.pallas_call(
@@ -289,9 +292,6 @@
         name="upper",
     )(pos, pat, front_in, lower_inv, u0, corner)
 
-    keep_col = (pos[1] * n_col + jnp.arange(n_col)) >= 2
-    keep_pat = jnp.where(keep_col[None, :], pat, 0).astype(BF)
-    pat_rows = jnp.pad(jnp.repeat(keep_pat, B, axis=0), ((0, 0), (0, 128 - n_col)))
     keep_spec = pl.BlockSpec((part, 128), lambda i: (i, 0))
     head_spec = pl.BlockSpec((part, head), lambda i: (i, 0))
     tail_spec = pl.BlockSpec((part, tail), lambda i: (i, 0))

time: 244 us -> 252 us (1.033); the launches traced: 243 us -> 247 us
  starting transfers between devices: 34.6 us -> 40.7 us
  waiting for transfers between devices: 103 us -> 97.6 us
  other arithmetic: 1.05 us -> 3.85 us
    ppermute x7, waiting for transfers between devices: 21.7 us -> 16.3 us  [scatter(): lax.ppermute(lower[c * rows:(c + 1) * rows], axis, [(0, c)])]
    ppermute x3, waiting for transfers between devices: 21.7 us -> 16.9 us  [tree(): block = block + lax.ppermute(block, axis, pairs)]
    ppermute x1, waiting for transfers between devices: 0.01 us -> 4.45 us  [local(): upper = plus(upper, lax.ppermute(upper, 'row', TREE[0]), made[1])]
    add x3, other arithmetic: 0.2 us -> 3.01 us  [tree(): block = block + lax.ppermute(block, axis, pairs)]
    ppermute x7, starting transfers between devices: 5.36 us -> 8.16 us  [scatter(): lax.ppermute(lower[c * rows:(c + 1) * rows], axis, [(0, c)])]
    unnamed x32 -> x42, local copies, waits for them, and re-layouts: 11.9 us -> 11.4 us
  transfers between devices with their start and end apart: 17 -> 17, of which waited for: 5 -> 6; matrix products, arithmetic and copies ran while one was open for 2% -> 2% of each run, Pallas kernels for 27% -> 27%
where the time goes in v3:
time: 252 us; the launch traced here: 247 us
  waiting for transfers between devices  97.6 us (39%)
  Pallas kernels  74.9 us (30%)
  starting transfers between devices  40.7 us (16%)
  local copies, waits for them, and re-layouts  16 us (6%)
  between operations  14.3 us (6%)
  other arithmetic  3.85 us (2%)
    all_to_all x3, waiting for transfers between devices, local(): lax.all_to_all(x, ('gz', 'row'), split_axis=0, concat_axis=0, tiled=True)  57.2 us
    all_to_all x3, starting transfers between devices, local(): lax.all_to_all(x, ('gz', 'row'), split_axis=0, concat_axis=0, tiled=True)  20.8 us
    pallas_call x2, Pallas kernels, local(): pl.pallas_call(add_kernel, grid=(8,), in_specs=[whole((1, slots)), whole(...  20.1 us
    pallas_call x2, Pallas kernels, pack_head(): pl.pallas_call(lambda *refs: pack_head_kernel(first, *refs), grid=(2,), i...  20 us
    ppermute x3, waiting for transfers between devices, tree(): block = block + lax.ppermute(block, axis, pairs)  16.9 us
    ppermute x7, waiting for transfers between devices, scatter(): lax.ppermute(lower[c * rows:(c + 1) * rows], axis, [(0, c)])  16.3 us
    pallas_call x1, Pallas kernels, local(): pl.pallas_call(update_kernel, grid=(4,), in_specs=[SMEM, whole((1, rows))...  14.3 us
    unnamed x42, local copies, waits for them, and re-layouts  11.4 us
  transfers between devices with their start and end apart: 17, of which 6 were waited for; matrix products, arithmetic and copies ran while one was open for 2% of the time, Pallas kernels for 27%

profile of v3, /device:TPU:96, one launch (start us, length us, event | category | flops | bytes accessed | tf_op | source)
XLA Modules:
  0.0 247.4 jit_solution(14429839921381784596)
XLA Ops:
  7.2 0.0 all-gather.2.cloned.1.call-start
  7.2 0.8 copy.15.pat_ref
  8.0 0.1 pad_add_fusion.pos_ref.refs_0_
  8.1 1.0 copy-done.1
  9.1 1.0 copy-done.5
  10.1 3.5 %panels_zero.1 = (bf16[2176,512]{1,0:T(8,128)(2,1)S(1)}, bf16[256,1024]{1,0:T(8,128)(2,1)S(1)}, bf16[512,256]{1,0:T(8,128)(2,1)}) custom-call(s32[2]{0:T(128)S(1)} %pad_add_fusion.pos_ref.refs_0_, s32[8,4]{1,0:T(8,128)S(1)} %copy.15.pat_ref, bf16[1,2048,1024]{2,1,0:T(8,128)(2,1)} %refs_1_.1, bf16[1,2048,1024]{2,1,0:T(8,128)(2,1)} %refs_1_.1, ...), custom_call_target="tpu_custom_call" | custom-call | flops 805306368 | bytes 6291456 | tf_op jit(solution)/shard_map/panels_zero/pallas_call | solution.py:264
  13.7 1.3 fusion
  15.0 0.7 collective-permute-start.6
  15.6 0.7 collective-permute-start.5
  16.3 1.4 collective-permute-start.4
  17.7 1.4 collective-permute-start.7
  19.1 1.4 collective-permute-start.3
  20.5 1.3 collective-permute-start.2
  21.8 1.8 add.23
  23.6 1.4 collective-permute-start.1
  25.0 1.4 collective-permute-start
  26.3 1.4 collective-permute-start.8
  27.7 0.1 select_convert_fusion
  27.8 0.1 copy.16
  27.9 0.1 broadcast_in_dim.24
  28.0 0.1 pad.4.refs_11_.refs_3_
  28.1 1.6 slots.1
  29.7 16.2 %collective-permute-done.2.refs_4_ = bf16[272,512]{1,0:T(8,128)(2,1)} collective-permute-done((bf16[272,512]{1,0:T(8,128)(2,1)}, bf16[272,512]{1,0:T(8,128)(2,1)}, u32[]{:S(2)}, u32[]{:S(2)}) %collective-permute-start.2) | collective-permute-done | bytes 278560 | tf_op jit(solution)/shard_map/ppermute | solution.py:225
  45.9 1.0 copy-done.8
  46.9 0.8 copy-done.9
  47.7 0.7 copy-done.13
  48.4 0.6 copy-done.16
  49.0 2.3 join.1.refs_4_
  51.4 1.1 add.24
  52.5 1.3 collective-permute-start.9
  53.8 16.9 %collective-permute-done.9 = bf16[512,256]{1,0:T(8,128)(2,1)S(1)} collective-permute-done((bf16[512,256]{1,0:T(8,128)(2,1)S(1)}, bf16[512,256]{1,0:T(8,128)(2,1)S(1)}, u32[]{:S(2)}, u32[]{:S(2)}) %collective-permute-start.9) | collective-permute-done | bytes 262176 | tf_op jit(solution)/shard_map/ppermute | solution.py:200
  70.7 0.1 add.25.corner_ref
  70.8 0.7 copy-done.12
  71.5 0.6 copy-done.17
  72.0 2.5 %upper.1.a_ref = bf16[576,1024]{1,0:T(8,128)(2,1)S(1)} custom-call(s32[2]{0:T(128)S(1)} %copy-done.17, s32[8,4]{1,0:T(8,128)S(1)} %copy-done.12, bf16[1,2048,1024]{2,1,0:T(8,128)(2,1)} %refs_1_.1, f32[1,2,256,256]{3,2,1,0:T(8,128)S(1)} %copy-done.2, bf16[256,1024]{1,0:T(8,128)(2,1)S(1)} %get-tuple-element.20.u0_ref, bf16[512,256]{1,0:T(8,128)(2,1)S(1)} %add.25.corner_ref), custom_call_target="tpu_custom_call" | custom-call | flops 536870912 | bytes 2097152 | tf_op jit(solution)/shard_map/upper/pallas_call | solution.py:284
  74.5 5.0 %collective-permute-start.10 = (bf16[576,1024]{1,0:T(8,128)(2,1)S(1)}, bf16[576,1024]{1,0:T(8,128)(2,1)S(1)}, u32[]{:S(2)}, u32[]{:S(2)}) collective-permute-start(bf16[576,1024]{1,0:T(8,128)(2,1)S(1)} %upper.1.a_ref), channel_id=1, source_target_pairs={{0,32},{1,33},{2,34},{3,35},{4,36},{5,37},{6,38},{7,39},{64,96},{6... | collective-permute-start | bytes 3538952 | tf_op jit(solution)/shard_map/ppermute | solution.py:329
  79.6 9.2 %pack_head.2 = (bf16[3072,768]{1,0:T(8,128)(2,1)}, bf16[3072,128]{1,0:T(8,128)(2,1)S(1)}, s32[8,3072]{1,0:T(8,128)S(1)}) custom-call(s32[1,2048]{1,0:T(1,128)S(1)} %copy-done.14, bf16[16,2048]{1,0:T(8,128)(2,1)S(1)} %copy-done.10, bf16[1,2048,1024]{2,1,0:T(8,128)(2,1)S(1)} %copy-done, bf16[2048,128]{1,0:T(8,128)(2,1)S(1)} %pad.4.refs_11_.refs_3_, ...), custom_call_target="tpu_custom_call" | custom-call | flops 8053063680 | bytes 8650752 | tf_op jit(solution)/shard_map/pack_head/pallas_call | solution.py:306
  88.7 4.4 %collective-permute-done.10.b_ref = bf16[576,1024]{1,0:T(8,128)(2,1)S(1)} collective-permute-done((bf16[576,1024]{1,0:T(8,128)(2,1)S(1)}, bf16[576,1024]{1,0:T(8,128)(2,1)S(1)}, u32[]{:S(2)}, u32[]{:S(2)}) %collective-permute-start.10) | collective-permute-done | bytes 1179680 | tf_op jit(solution)/shard_map/ppermute | solution.py:329
  93.2 0.3 plus.3.refs_4_.a_ref
  93.4 1.4 collective-permute-start.11
  94.8 10.9 %pack_head.3 = (bf16[3072,768]{1,0:T(8,128)(2,1)}, bf16[3072,128]{1,0:T(8,128)(2,1)S(1)}, s32[8,3072]{1,0:T(8,128)S(1)}) custom-call(s32[1,2048]{1,0:T(1,128)S(1)} %copy-done.14, bf16[16,2048]{1,0:T(8,128)(2,1)S(1)} %copy-done.10, bf16[1,2048,1024]{2,1,0:T(8,128)(2,1)} %refs_1_.1, ...), custom_call_target="tpu_custom_call", output_to_operand_aliasing={{0}: (5, {}), {1}: (6, {}), {2}: (7, {})} | custom-call | flops 8053063680 | bytes 8650752 | tf_op jit(solution)/shard_map/pack_head/pallas_call | solution.py:306
  105.7 2.8 %collective-permute-done.11.b_ref = bf16[576,1024]{1,0:T(8,128)(2,1)S(1)} collective-permute-done((bf16[576,1024]{1,0:T(8,128)(2,1)S(1)}, bf16[576,1024]{1,0:T(8,128)(2,1)S(1)}, u32[]{:S(2)}, u32[]{:S(2)}) %collective-permute-start.11) | collective-permute-done | bytes 1179680 | tf_op jit(solution)/shard_map/ppermute | solution.py:332
  108.4 0.3 plus.4.a_ref
  108.7 1.4 collective-permute-start.12
  110.1 0.7 all_to_all.12
  110.8 9.5 %all-to-all-start = ((s32[32,1,96]{2,1,0:T(1,128)}), s32[32,1,96]{2,1,0:T(1,128)S(1)}, u32[]{:S(2)}, u32[]{:S(2)}) async-start(s32[32,1,96]{2,1,0:T(1,128)} %bitcast.6), calls=%async_computation | async-start | bytes 32768 | tf_op jit(solution)/shard_map/all_to_all | solution.py:249
  120.3 1.0 copy-done.3
  121.3 1.3 copy-done.4
  122.6 0.3 plus.5.u_ref.refs_1_
  122.9 1.0 copy-done.6
  124.0 1.6 copy-done.19
  125.6 14.3 %update_head.1 = (bf16[3072,768]{1,0:T(8,128)(2,1)}, bf16[3072,512]{1,0:T(8,128)(2,1)}, bf16[2048,512]{1,0:T(8,128)(2,1)}) custom-call(s32[2]{0:T(128)S(1)} %copy-done.18, s32[1,2048]{1,0:T(1,128)S(1)} %copy-done.14, bf16[2176,512]{1,0:T(8,128)(2,1)S(1)} %copy-done.19, f32[1,2,256,256]{3,2,1,0:T(8,128)S(1)} %copy-done.6, ...), custom_call_target="tpu_custom_call" | custom-call | flops 8858370048 | bytes 9437184 | tf_op jit(solution)/shard_map/update_head/pallas_call | solution.py:336
  139.9 7.3 %all-to-all-start.2 = ((bf16[32,96,768]{2,1,0:T(8,128)(2,1)}), bf16[32,96,768]{2,1,0:T(8,128)(2,1)}, u32[]{:S(2)}, u32[]{:S(2)}) async-start(bf16[32,96,768]{2,1,0:T(8,128)(2,1)} %bitcast.14), calls=%async_computation.2 | async-start | bytes 9437184 | tf_op jit(solution)/shard_map/all_to_all | solution.py:249
  147.2 5.2 %pack_tail.1.refs_2_ = bf16[3072,256]{1,0:T(8,128)(2,1)S(1)} custom-call(s32[1,2048]{1,0:T(1,128)S(1)} %copy-done.14, bf16[1,2048,1024]{2,1,0:T(8,128)(2,1)} %refs_1_.1, bf16[3072,128]{1,0:T(8,128)(2,1)S(1)} %get-tuple-element.25.refs_0_.keep_ref.refs_2_.refs_3_, bf16[3072,768]{1,0:T(8,128)(2,1)} %get-tuple-element.30.refs_3_), custom_call_target="tpu_custom_call" | custom-call | flops 6442450944 | bytes 2621440 | tf_op jit(solution)/shard_map/pack_tail/pallas_call | solution.py:359
  152.4 4.6 %update_tail.1 = bf16[3072,256]{1,0:T(8,128)(2,1)} custom-call(bf16[3072,512]{1,0:T(8,128)(2,1)} %get-tuple-element.29.refs_0_, bf16[576,1024]{1,0:T(8,128)(2,1)S(1)} %plus.5.u_ref.refs_1_, bf16[3072,256]{1,0:T(8,128)(2,1)S(1)} %pack_tail.1.refs_2_, bf16[3072,128]{1,0:T(8,128)(2,1)S(1)} %get-tuple-element.25.refs_0_.keep_ref.refs_2_.refs_3_), custom_call_target="tpu_custom_call" | custom-call | flops 805306368 | bytes 6291456 | tf_op jit(solution)/shard_map/update_tail/pallas_call | solution.py:374
  157.0 49.9 %all-to-all-done.2 = bf16[32,96,768]{2,1,0:T(8,128)(2,1)} async-done(((bf16[32,96,768]{2,1,0:T(8,128)(2,1)}), bf16[32,96,768]{2,1,0:T(8,128)(2,1)}, u32[]{:S(2)}, u32[]{:S(2)}) %all-to-all-start.2) | async-done | bytes 4718624 | tf_op jit(solution)/shard_map/all_to_all | solution.py:249
  206.9 4.0 %all-to-all-start.1 = ((bf16[32,96,256]{2,1,0:T(8,128)(2,1)}), bf16[32,96,256]{2,1,0:T(8,128)(2,1)S(1)}, u32[]{:S(2)}, u32[]{:S(2)}) async-start(bf16[32,96,256]{2,1,0:T(8,128)(2,1)} %bitcast.7), calls=%async_computation.1 | async-start | bytes 3145728 | tf_op jit(solution)/shard_map/all_to_all | solution.py:249
  210.9 0.5 broadcast.21
  211.4 0.7 reduce.7
  212.1 0.1 reshape.34.index_ref
  212.2 1.0 slice_bitcast_fusion
  213.2 14.4 %add_head.1.refs_0_ = f32[2048,1024]{1,0:T(8,128)} custom-call(s32[1,3072]{1,0:T(1,128)S(1)} %reshape.34.index_ref, bf16[3072,768]{1,0:T(8,128)(2,1)} %bitcast.10.got_ref), custom_call_target="tpu_custom_call" | custom-call | flops 9663676416 | bytes 15728640 | tf_op jit(solution)/shard_map/add_head/pallas_call | solution.py:386
  227.6 7.2 %all-to-all-done.1 = bf16[32,96,256]{2,1,0:T(8,128)(2,1)S(1)} async-done(((bf16[32,96,256]{2,1,0:T(8,128)(2,1)}), bf16[32,96,256]{2,1,0:T(8,128)(2,1)S(1)}, u32[]{:S(2)}, u32[]{:S(2)}) %all-to-all-start.1) | async-done | bytes 1572896 | tf_op jit(solution)/shard_map/all_to_all | solution.py:249
  234.8 5.7 %add_tail.1 = f32[2048,1024]{1,0:T(8,128)} custom-call(s32[1,3072]{1,0:T(1,128)S(1)} %reshape.34.index_ref, bf16[3072,256]{1,0:T(8,128)(2,1)S(1)} %bitcast.13, f32[2048,1024]{1,0:T(8,128)} %add_head.1.refs_0_), custom_call_target="tpu_custom_call", output_to_operand_aliasing={{}: (2, {})} | custom-call | flops 6442450944 | bytes 5242880 | tf_op jit(solution)/shard_map/add_tail/pallas_call | solution.py:396
  (44 shorter events, 0.2 us)
Async XLA Ops:
  7.2 115.7 %all-gather.2.cloned.1.call-start = ((), (), s32[]{:S(2)}) async-start(), calls=%async_computation.3 | async-start | bytes 2506752 | tf_op jit(solution)/shard_map/all_gather | solution.py:282
  8.0 5.7 %copy-start.11 = (s32[8,4]{1,0:T(8,128)}, s32[8,4]{1,0:T(8,128)S(1)}, u32[]{:S(2)}) copy-start(s32[8,4]{1,0:T(8,128)S(1)} %copy.15.pat_ref) | copy-start | bytes 388
  8.1 1.0 copy-start.1
  9.1 1.0 copy-start.5
  10.1 3.5 %copy-start.15 = (s32[2]{0:T(128)}, s32[2]{0:T(128)S(1)}, u32[]{:S(2)}) copy-start(s32[2]{0:T(128)S(1)} %pad_add_fusion.pos_ref.refs_0_) | copy-start | bytes 28
  13.7 14.0 %copy-start.20 = (s32[1,8,4]{1,2,0:T(4,128)S(1)}, s32[1,8,4]{1,2,0:T(4,128)}, u32[]{:S(2)}) copy-start(s32[1,8,4]{1,2,0:T(4,128)} %param.6) | copy-start | bytes 388
  15.0 8.6 %collective-permute-start.6 = (bf16[272,512]{1,0:T(8,128)(2,1)}, bf16[272,512]{1,0:T(8,128)(2,1)S(1)}, u32[]{:S(2)}, u32[]{:S(2)}) collective-permute-start(bf16[272,512]{1,0:T(8,128)(2,1)} %get-tuple-element.31), channel_id=1, source_target_pairs={{0,7},{8,15},{16,23},{24,31},{32,39},{40,47},{48,55},{56,63},{64,7... | collective-permute-start | bytes 835592 | tf_op jit(solution)/shard_map/ppermute | solution.py:225
  15.6 9.3 %collective-permute-start.5 = (bf16[272,512]{1,0:T(8,128)(2,1)}, bf16[272,512]{1,0:T(8,128)(2,1)S(1)}, u32[]{:S(2)}, u32[]{:S(2)}) collective-permute-start(bf16[272,512]{1,0:T(8,128)(2,1)} %get-tuple-element.32), channel_id=1, source_target_pairs={{0,6},{8,14},{16,22},{24,30},{32,38},{40,46},{48,54},{56,62},{64,7... | collective-permute-start | bytes 835592 | tf_op jit(solution)/shard_map/ppermute | solution.py:225
  16.3 10.0 %collective-permute-start.4 = (bf16[272,512]{1,0:T(8,128)(2,1)}, bf16[272,512]{1,0:T(8,128)(2,1)}, u32[]{:S(2)}, u32[]{:S(2)}) collective-permute-start(bf16[272,512]{1,0:T(8,128)(2,1)} %get-tuple-element.33), channel_id=1, source_target_pairs={{0,5},{8,13},{16,21},{24,29},{32,37},{40,45},{48,53},{56,61},{64,6... | collective-permute-start | bytes 835592 | tf_op jit(solution)/shard_map/ppermute | solution.py:225
  17.7 2.8 %collective-permute-start.7 = (bf16[512,256]{1,0:T(8,128)(2,1)}, bf16[512,256]{1,0:T(8,128)(2,1)}, u32[]{:S(2)}, u32[]{:S(2)}) collective-permute-start(bf16[512,256]{1,0:T(8,128)(2,1)} %get-tuple-element.21), channel_id=1, source_target_pairs={{0,4},{8,12},{16,20},{24,28},{32,36},{40,44},{48,52},{56,60},{64,6... | collective-permute-start | bytes 786440 | tf_op jit(solution)/shard_map/ppermute | solution.py:200
  19.1 10.6 %collective-permute-start.3 = (bf16[272,512]{1,0:T(8,128)(2,1)}, bf16[272,512]{1,0:T(8,128)(2,1)}, u32[]{:S(2)}, u32[]{:S(2)}) collective-permute-start(bf16[272,512]{1,0:T(8,128)(2,1)} %get-tuple-element.34), channel_id=1, source_target_pairs={{0,4},{8,12},{16,20},{24,28},{32,36},{40,44},{48,52},{56,60},{64,6... | collective-permute-start | bytes 835592 | tf_op jit(solution)/shard_map/ppermute | solution.py:225
  20.5 25.5 %collective-permute-start.2 = (bf16[272,512]{1,0:T(8,128)(2,1)}, bf16[272,512]{1,0:T(8,128)(2,1)}, u32[]{:S(2)}, u32[]{:S(2)}) collective-permute-start(bf16[272,512]{1,0:T(8,128)(2,1)} %get-tuple-element.35), channel_id=1, source_target_pairs={{0,3},{8,11},{16,19},{24,27},{32,35},{40,43},{48,51},{56,59},{64,6... | collective-permute-start | bytes 835592 | tf_op jit(solution)/shard_map/ppermute | solution.py:225
  23.6 22.4 %collective-permute-start.1 = (bf16[272,512]{1,0:T(8,128)(2,1)}, bf16[272,512]{1,0:T(8,128)(2,1)}, u32[]{:S(2)}, u32[]{:S(2)}) collective-permute-start(bf16[272,512]{1,0:T(8,128)(2,1)} %get-tuple-element.36), channel_id=1, source_target_pairs={{0,2},{8,10},{16,18},{24,26},{32,34},{40,42},{48,50},{56,58},{64,6... | collective-permute-start | bytes 835592 | tf_op jit(solution)/shard_map/ppermute | solution.py:225
  25.0 3.0 %copy-start.7 = (bf16[272,512]{1,0:T(8,128)(2,1)}, bf16[272,512]{1,0:T(8,128)(2,1)S(1)}, u32[]{:S(2)}) copy-start(bf16[272,512]{1,0:T(8,128)(2,1)S(1)} %collective-permute-done.5.refs_7_) | copy-start | bytes 835588
  25.0 21.0 %collective-permute-start = (bf16[272,512]{1,0:T(8,128)(2,1)}, bf16[272,512]{1,0:T(8,128)(2,1)}, u32[]{:S(2)}, u32[]{:S(2)}) collective-permute-start(bf16[272,512]{1,0:T(8,128)(2,1)} %get-tuple-element.37), channel_id=1, source_target_pairs={{0,1},{8,9},{16,17},{24,25},{32,33},{40,41},{48,49},{56,57},{64,65... | collective-permute-start | bytes 835592 | tf_op jit(solution)/shard_map/ppermute | solution.py:225
  26.3 25.0 %collective-permute-start.8 = (bf16[512,256]{1,0:T(8,128)(2,1)}, bf16[512,256]{1,0:T(8,128)(2,1)}, u32[]{:S(2)}, u32[]{:S(2)}) collective-permute-start(bf16[512,256]{1,0:T(8,128)(2,1)} %add.23), channel_id=1, source_target_pairs={{0,2},{4,6},{8,10},{12,14},{16,18},{20,22},{24,26},{28,30},{32,34}... | collective-permute-start | bytes 786440 | tf_op jit(solution)/shard_map/ppermute | solution.py:200
  45.9 1.0 copy-start.8
  46.9 0.8 copy-start.9
  47.7 0.7 copy-start.13
  48.4 0.6 copy-start.16
  51.3 19.5 %copy-start.2 = (f32[1,2,256,256]{3,2,1,0:T(8,128)S(1)}, f32[1,2,256,256]{3,2,1,0:T(8,128)}, u32[]{:S(2)}) copy-start(f32[1,2,256,256]{3,2,1,0:T(8,128)} %li_ref.3) | copy-start | bytes 1572868
  52.5 18.2 %collective-permute-start.9 = (bf16[512,256]{1,0:T(8,128)(2,1)S(1)}, bf16[512,256]{1,0:T(8,128)(2,1)S(1)}, u32[]{:S(2)}, u32[]{:S(2)}) collective-permute-start(bf16[512,256]{1,0:T(8,128)(2,1)S(1)} %add.24), channel_id=1, source_target_pairs={{0,1},{2,3},{4,5},{6,7},{8,9},{10,11},{12,13},{14,15},{16,17},{18,... | collective-permute-start | bytes 786440 | tf_op jit(solution)/shard_map/ppermute | solution.py:200
  70.8 0.7 copy-start.12
  71.5 0.6 copy-start.17
  72.0 7.5 %copy-start = (bf16[1,2048,1024]{2,1,0:T(8,128)(2,1)S(1)}, bf16[1,2048,1024]{2,1,0:T(8,128)(2,1)}, u32[]{:S(2)}) copy-start(bf16[1,2048,1024]{2,1,0:T(8,128)(2,1)} %refs_1_.1) | copy-start | bytes 12582916
  72.0 7.5 %copy-start.10 = (bf16[16,2048]{1,0:T(8,128)(2,1)S(1)}, bf16[16,2048]{1,0:T(8,128)(2,1)}, u32[]{:S(2)}) copy-start(bf16[16,2048]{1,0:T(8,128)(2,1)} %get-tuple-element.19.refs_10_.refs_1_) | copy-start | bytes 196612
  72.0 7.5 %copy-start.14 = (s32[1,2048]{1,0:T(1,128)S(1)}, s32[1,2048]{1,0:T(1,128)}, u32[]{:S(2)}) copy-start(s32[1,2048]{1,0:T(1,128)} %get-tuple-element.17.refs_9_.refs_0_.slot_ref) | copy-start | bytes 24580
  74.5 18.6 %collective-permute-start.10 = (bf16[576,1024]{1,0:T(8,128)(2,1)S(1)}, bf16[576,1024]{1,0:T(8,128)(2,1)S(1)}, u32[]{:S(2)}, u32[]{:S(2)}) collective-permute-start(bf16[576,1024]{1,0:T(8,128)(2,1)S(1)} %upper.1.a_ref), channel_id=1, source_target_pairs={{0,32},{1,33},{2,34},{3,35},{4,36},{5,37},{6,38},{7,39},{64,96},{6... | collective-permute-start | bytes 3538952 | tf_op jit(solution)/shard_map/ppermute | solution.py:329
  93.4 15.0 %collective-permute-start.11 = (bf16[576,1024]{1,0:T(8,128)(2,1)S(1)}, bf16[576,1024]{1,0:T(8,128)(2,1)S(1)}, u32[]{:S(2)}, u32[]{:S(2)}) collective-permute-start(bf16[576,1024]{1,0:T(8,128)(2,1)S(1)} %plus.3.refs_4_.a_ref), channel_id=1, source_target_pairs={{0,16},{32,48},{1,17},{33,49},{2,18},{34,50},{3,19},{35,51},{4,20}... | collective-permute-start | bytes 3538952 | tf_op jit(solution)/shard_map/ppermute | solution.py:332
  108.7 14.2 %copy-start.18 = (s32[2]{0:T(128)S(1)}, s32[2]{0:T(128)}, u32[]{:S(2)}) copy-start(s32[2]{0:T(128)} %copy-done.15) | copy-start | bytes 28
  108.7 11.6 %collective-permute-start.12 = (bf16[576,1024]{1,0:T(8,128)(2,1)S(1)}, bf16[576,1024]{1,0:T(8,128)(2,1)S(1)}, u32[]{:S(2)}, u32[]{:S(2)}) collective-permute-start(bf16[576,1024]{1,0:T(8,128)(2,1)S(1)} %plus.4.a_ref), channel_id=1, source_target_pairs={{0,8},{16,24},{32,40},{48,56},{1,9},{17,25},{33,41},{49,57},{2,10}... | collective-permute-start | bytes 3538952 | tf_op jit(solution)/shard_map/ppermute | solution.py:333
  110.8 29.0 %all-to-all-start = ((s32[32,1,96]{2,1,0:T(1,128)}), s32[32,1,96]{2,1,0:T(1,128)S(1)}, u32[]{:S(2)}, u32[]{:S(2)}) async-start(s32[32,1,96]{2,1,0:T(1,128)} %bitcast.6), calls=%async_computation | async-start | bytes 32768 | tf_op jit(solution)/shard_map/all_to_all | solution.py:249
  120.3 1.0 copy-start.3
  121.3 1.3 copy-start.4
  122.9 1.0 copy-start.6
  124.0 1.6 copy-start.19
  139.9 67.1 %all-to-all-start.2 = ((bf16[32,96,768]{2,1,0:T(8,128)(2,1)}), bf16[32,96,768]{2,1,0:T(8,128)(2,1)}, u32[]{:S(2)}, u32[]{:S(2)}) async-start(bf16[32,96,768]{2,1,0:T(8,128)(2,1)} %bitcast.14), calls=%async_computation.2 | async-start | bytes 9437184 | tf_op jit(solution)/shard_map/all_to_all | solution.py:249
  206.9 27.9 %all-to-all-start.1 = ((bf16[32,96,256]{2,1,0:T(8,128)(2,1)}), bf16[32,96,256]{2,1,0:T(8,128)(2,1)S(1)}, u32[]{:S(2)}, u32[]{:S(2)}) async-start(bf16[32,96,256]{2,1,0:T(8,128)(2,1)} %bitcast.7), calls=%async_computation.1 | async-start | bytes 3145728 | tf_op jit(solution)/shard_map/all_to_all | solution.py:249
Sparse Core Ops, SparseCore 0:
  51.5 50.0 all-gather.1
